TPU v7x, 128 devices: a whole 4x4x4 slice. The times are simulated.
128 devices in a mesh: row: 8 (over x_lo, y), col: 16 (over x_hi, z, core).
Axes of the slice: x: 4 (x_hi: 2, x_lo: 2; x = x_hi * 2 + x_lo), y: 4, z: 4, core: 2. Of those that a mesh axis runs over, the one named last changes fastest.
Arguments:
- latent: bfloat16 [8, 64, 64, 640], P(None, 'row', 'col'), may hold values from -6 to 6
- gn1_gain: float32 [640], replicated, may hold values from 0.5 to 1.5
- gn1_bias: float32 [640], replicated, may hold values from -1.75 to 1.75
- conv1_weight: bfloat16 [3, 3, 640, 640], replicated, may hold values from -0.078125 to 0.078125
- conv1_bias: float32 [640], replicated, may hold values from -1.75 to 1.75
- time_shift: float32 [8, 640], replicated, may hold values from -6 to 6
- gn2_gain: float32 [640], replicated, may hold values from 0.5 to 1.5
- gn2_bias: float32 [640], replicated, may hold values from -1.75 to 1.75
- conv2_weight: bfloat16 [3, 3, 640, 640], replicated, may hold values from -0.078125 to 0.078125
- conv2_bias: float32 [640], replicated, may hold values from -1.75 to 1.75
- gn3_gain: float32 [640], replicated, may hold values from 0.5 to 1.5
- gn3_bias: float32 [640], replicated, may hold values from -1.75 to 1.75
- in_weight: bfloat16 [640, 640], replicated, may hold values from -0.25 to 0.25
- in_bias: float32 [640], replicated, may hold values from -1.75 to 1.75
- ln_gain: float32 [640], replicated, may hold values from 0.5 to 1.5
- ln_bias: float32 [640], replicated, may hold values from -1.75 to 1.75
- query_weight: bfloat16 [640, 640], replicated, may hold values from -0.5 to 0.5
- key_weight: bfloat16 [640, 640], replicated, may hold values from -0.5 to 0.5
- value_weight: bfloat16 [640, 640], replicated, may hold values from -0.25 to 0.25
- out_weight: bfloat16 [640, 640], replicated, may hold values from -0.25 to 0.25
- out_bias: float32 [640], replicated, may hold values from -1.75 to 1.75
- proj_weight: bfloat16 [640, 640], replicated, may hold values from -0.25 to 0.25
- proj_bias: float32 [640], replicated, may hold values from -1.75 to 1.75
Outputs:
- block_out: bfloat16 [8, 64, 64, 640], P('row', None, 'col')
All inputs are finite; a program needn't handle non-finite values.
Results may differ from a plain program's by a relative error of at most 0.024.
Values may be sent and summed in bfloat16 or wider, within the bound.
A program may use at most 192 MiB of HBM per device.

v0:
```python
import jax
import jax.numpy as jnp
from jax import lax
from jax.sharding import PartitionSpec as P

HEADS = 10
HEAD_DIM = 64
GROUPS = 32


def with_halo(block, sides, width):
    for axis, dim in sides:
        count = lax.axis_size(axis)
        forward = [(i, i + 1) for i in range(count - 1)]
        backward = [(target, source) for source, target in forward]
        low = lax.ppermute(
            lax.slice_in_dim(block, block.shape[dim] - width, None, axis=dim), axis, forward
        )
        high = lax.ppermute(lax.slice_in_dim(block, 0, width, axis=dim), axis, backward)
        block = jnp.concatenate([low, block, high], axis=dim)
    return block


def moments(values, groups):
    images, height, breadth, channels = values.shape
    grouped = values.reshape(images, height * breadth, groups, channels // groups)
    return (jnp.sum(grouped, axis=(1, 3)), jnp.sum(grouped * grouped, axis=(1, 3)))


def normalize(values, first_sum, second_sum, cells, gain_vec, bias_vec, epsilon):
    average = first_sum / cells
    variance = second_sum / cells - average * average
    inverse = lax.rsqrt(variance + epsilon)
    group_size = values.shape[-1] // first_sum.shape[-1]
    average_c = jnp.repeat(average, group_size, axis=1)[:, None, None, :]
    inverse_c = jnp.repeat(inverse, group_size, axis=1)[:, None, None, :]
    return (values - average_c) * inverse_c * gain_vec + bias_vec


def tile_norm(values, gain_vec, bias_vec, epsilon, cells):
    first_sum, second_sum = moments(values, GROUPS)
    totals = lax.psum((first_sum, second_sum), ("row", "col"))
    return normalize(values, totals[0], totals[1], cells, gain_vec, bias_vec, epsilon)


def convolve(activation, weight, bias_vec):
    images, height, breadth, channels = activation.shape
    padded = with_halo(activation, (("row", 1), ("col", 2)), 1)
    summed = jnp.zeros((images * height * breadth, weight.shape[3]), jnp.float32)
    for shift_row in range(3):
        for shift_col in range(3):
            window = padded[:, shift_row : shift_row + height, shift_col : shift_col + breadth, :]
            summed = summed + jnp.dot(
                window.reshape(-1, channels),
                weight[shift_row, shift_col],
                preferred_element_type=jnp.float32,
            )
    return summed.reshape(images, height, breadth, -1) + bias_vec


def layer_norm(values, gain_vec, bias_vec):
    average = jnp.mean(values, axis=-1, keepdims=True)
    centered = values - average
    variance = jnp.mean(centered * centered, axis=-1, keepdims=True)
    return centered * lax.rsqrt(variance + 1e-05) * gain_vec + bias_vec


def absorb(running, query_heads, key_part, value_part):
    row_max, row_sum, accum = running
    key_heads = key_part.reshape(-1, HEADS, HEAD_DIM)
    value_heads = value_part.reshape(-1, HEADS, HEAD_DIM)
    scores = jnp.einsum(
        "qhd,khd->hqk", query_heads, key_heads, preferred_element_type=jnp.float32
    ) * HEAD_DIM ** (-0.5)
    new_max = jnp.maximum(row_max, jnp.max(scores, axis=-1))
    factor = jnp.exp(row_max - new_max)
    expo = jnp.exp(scores - new_max[:, :, None])
    new_sum = jnp.sum(expo, axis=-1)
    weighted = jnp.einsum(
        "hqk,khd->qhd", expo.astype(jnp.bfloat16), value_heads, preferred_element_type=jnp.float32
    )
    weighted = weighted.reshape(weighted.shape[0], HEADS * HEAD_DIM)
    new_accum = accum * jnp.repeat(factor.T, HEAD_DIM, axis=1) + weighted
    return (new_max, new_sum, new_accum)


def shards(
    latent,
    gn1_gain,
    gn1_bias,
    conv1_weight,
    conv1_bias,
    time_shift,
    gn2_gain,
    gn2_bias,
    conv2_weight,
    conv2_bias,
    gn3_gain,
    gn3_bias,
    in_weight,
    in_bias,
    ln_gain,
    ln_bias,
    query_weight,
    key_weight,
    value_weight,
    out_weight,
    out_bias,
    proj_weight,
    proj_bias,
):
    images, height, breadth, channels = latent.shape
    image_cells = height * lax.axis_size("row") * breadth * lax.axis_size("col")
    group_cells = image_cells * (channels // GROUPS)
    source = latent.astype(jnp.float32)
    first_act = jax.nn.silu(tile_norm(source, gn1_gain, gn1_bias, 1e-05, group_cells)).astype(
        jnp.bfloat16
    )
    first_conv = convolve(first_act, conv1_weight, conv1_bias) + time_shift[:, None, None, :]
    second_act = jax.nn.silu(tile_norm(first_conv, gn2_gain, gn2_bias, 1e-05, group_cells)).astype(
        jnp.bfloat16
    )
    resnet_out = (source + convolve(second_act, conv2_weight, conv2_bias)).astype(jnp.bfloat16)
    strip = lax.all_to_all(resnet_out, "row", split_axis=0, concat_axis=1, tiled=True)
    strip_f32 = strip.astype(jnp.float32)
    whole_first, whole_second = moments(resnet_out.astype(jnp.float32), GROUPS)
    totals = lax.psum((whole_first, whole_second), ("row", "col"))
    mine = lax.axis_index("row")
    first_sum = lax.dynamic_slice_in_dim(totals[0], mine, 1, 0)
    second_sum = lax.dynamic_slice_in_dim(totals[1], mine, 1, 0)
    attn_in = normalize(
        strip_f32, first_sum, second_sum, group_cells, gn3_gain, gn3_bias, 1e-06
    ).astype(jnp.bfloat16)
    flat = attn_in.reshape(-1, channels)
    inner = (jnp.dot(flat, in_weight, preferred_element_type=jnp.float32) + in_bias).astype(
        jnp.bfloat16
    )
    normed = layer_norm(inner.astype(jnp.float32), ln_gain, ln_bias).astype(jnp.bfloat16)
    queries = jnp.dot(normed, query_weight, preferred_element_type=jnp.float32).astype(jnp.bfloat16)
    query_heads = queries.reshape(-1, HEADS, HEAD_DIM)
    local_tokens = flat.shape[0]
    strip_rows = strip.shape[1]
    starting = (
        jnp.full((HEADS, local_tokens), -1e30, jnp.float32),
        jnp.zeros((HEADS, local_tokens), jnp.float32),
        jnp.zeros((local_tokens, channels), jnp.float32),
    )
    keys = (
        jnp.dot(normed, key_weight, preferred_element_type=jnp.float32)
        .astype(jnp.bfloat16)
        .reshape(strip_rows, breadth, channels)
    )
    values = (
        jnp.dot(normed, value_weight, preferred_element_type=jnp.float32)
        .astype(jnp.bfloat16)
        .reshape(strip_rows, breadth, channels)
    )
    finished = absorb(
        starting,
        query_heads,
        lax.all_gather(keys, "col", axis=1, tiled=True).reshape(-1, channels),
        lax.all_gather(values, "col", axis=1, tiled=True).reshape(-1, channels),
    )
    row_max, row_sum, accum = finished
    attended = (accum / jnp.repeat(row_sum.T, HEAD_DIM, axis=1)).astype(jnp.bfloat16)
    mixed = (
        inner.astype(jnp.float32)
        + jnp.dot(attended, out_weight, preferred_element_type=jnp.float32)
        + out_bias
    ).astype(jnp.bfloat16)
    projected = jnp.dot(mixed, proj_weight, preferred_element_type=jnp.float32) + proj_bias
    return (strip_f32 + projected.reshape(strip.shape)).astype(jnp.bfloat16)


def solution(mesh):
    placed = (
        P(None, "row", "col", None),
        P(),
        P(),
        P(),
        P(),
        P(),
        P(),
        P(),
        P(),
        P(),
        P(),
        P(),
        P(),
        P(),
        P(),
        P(),
        P(),
        P(),
        P(),
        P(),
        P(),
        P(),
        P(),
    )
    return jax.shard_map(
        shards, mesh=mesh, in_specs=placed, out_specs=P("row", None, "col", None), check_vma=False
    )
```

profile of v0, /device:TPU:1, one launch (start us, length us, event | category | flops | bytes accessed | tf_op | source)
XLA Modules:
  0.0 560.5 jit_solution(10996362018720124102)
XLA Ops:
  8.4 68.8 %all-reduce.2 = (f32[8,32]{1,0:T(8,128)S(1)}, f32[8,32]{1,0:T(8,128)S(1)}) all-reduce(f32[8,32]{1,0:T(8,128)S(1)} %reduce_sum.114, f32[8,32]{1,0:T(8,128)S(1)} %reduce_sum.94), channel_id=1, replica_groups=mesh['row'=8,'col'=16] {'row','col'}, use_global_device_ids=true, to_apply=%region_5.6 | all-reduce | flops 512 | bytes 4096 | tf_op jit(solution)/shard_map/psum | solution.py:42
  80.6 4.0 collective-permute-start
  88.7 2.7 collective-permute-start.2
  91.4 2.0 collective-permute-start.3
  95.5 3.3 collective-permute-done.3
  105.5 1.8 reshape.190
  107.3 1.8 reshape.191
  125.7 3.3 fusion.4
  129.1 80.6 %all-reduce.1 = (f32[8,32]{1,0:T(8,128)S(1)}, f32[8,32]{1,0:T(8,128)S(1)}) all-reduce(f32[8,32]{1,0:T(8,128)S(1)} %copy.46, f32[8,32]{1,0:T(8,128)S(1)} %copy.45), channel_id=1, replica_groups=mesh['row'=8,'col'=16] {'row','col'}, use_global_device_ids=true, to_apply=%region_9.10 | all-reduce | flops 512 | bytes 4096 | tf_op jit(solution)/shard_map/psum | solution.py:42
  213.1 4.0 collective-permute-start.4
  222.0 4.5 collective-permute-start.6
  226.5 1.9 collective-permute-start.7
  230.5 3.4 collective-permute-done.7
  233.9 1.8 maximum_maximum_fusion.1
  237.6 2.6 fusion.23
  243.1 1.8 reshape.201
  244.9 1.8 reshape.202
  246.7 1.8 reshape.203
  250.3 1.9 convolution_add_fusion.9
  263.8 3.4 all-to-all-start
  267.8 71.2 %all-reduce = (f32[8,32]{1,0:T(8,128)S(1)}, f32[8,32]{1,0:T(8,128)S(1)}) all-reduce(f32[8,32]{1,0:T(8,128)S(1)} %reduce_sum.122, f32[8,32]{1,0:T(8,128)S(1)} %reduce_sum.119), channel_id=1, replica_groups=mesh['row'=8,'col'=16] {'row','col'}, use_global_device_ids=true, to_apply=%region_15.16 | all-reduce | flops 512 | bytes 4096 | tf_op jit(solution)/shard_map/psum | solution.py:127
  347.3 53.5 %all-gather.5.cloned.1.call-done = bf16[64,64,640]{2,0,1:T(8,128)(2,1)} async-done(((bf16[64,4,640]{2,0,1:T(8,128)(2,1)}), bf16[64,64,640]{2,0,1:T(8,128)(2,1)}) %all-gather.5.cloned.1.call-update) | async-done | bytes 5242896 | tf_op jit(solution)/shard_map/all_gather | solution.py:162
  400.8 19.0 %copy.51 = bf16[64,64,640]{1,0,2:T(8,128)(2,1)} copy(bf16[64,64,640]{2,0,1:T(8,128)(2,1)} %all-gather.5.cloned.1.call-done) | data formatting | bytes 10485760 | tf_op jit(solution)/shard_map/all_gather | solution.py:162
  419.8 14.5 %reshape_reshape.7 = bf16[4096,10,64]{0,2,1:T(8,128)(2,1)} reshape(bf16[64,64,640]{1,0,2:T(8,128)(2,1)} %copy.51) | data formatting | bytes 10485760 | tf_op jit(solution)/shard_map/reshape;reshape | solution.py:71
  434.4 26.6 %all-gather.3.cloned.1.call-done = bf16[64,64,640]{2,0,1:T(8,128)(2,1)} async-done(((bf16[64,4,640]{2,0,1:T(8,128)(2,1)}), bf16[64,64,640]{2,0,1:T(8,128)(2,1)}) %all-gather.3.cloned.1.call-update) | async-done | bytes 5242896 | tf_op jit(solution)/shard_map/all_gather | solution.py:161
  461.0 19.0 %copy.49 = bf16[64,64,640]{1,0,2:T(8,128)(2,1)} copy(bf16[64,64,640]{2,0,1:T(8,128)(2,1)} %all-gather.3.cloned.1.call-done) | data formatting | bytes 10485760 | tf_op jit(solution)/shard_map/all_gather | solution.py:161
  480.0 14.6 %reshape_reshape.6 = bf16[4096,10,64]{0,2,1:T(8,128)(2,1)} reshape(bf16[64,64,640]{1,0,2:T(8,128)(2,1)} %copy.49) | data formatting | bytes 10485760 | tf_op jit(solution)/shard_map/reshape;reshape | solution.py:70
  494.6 18.9 %multiply_reduce_fusion = (f32[10,256]{1,0:T(8,128)S(1)}, f32[10,256,4096]{2,1,0:T(8,128)}) fusion(bf16[256,10,64]{0,2,1:T(8,128)(2,1)S(1)} %bitcast.115, bf16[4096,10,64]{0,2,1:T(8,128)(2,1)} %reshape_reshape.6), kind=kOutput, calls=%fused_computation.1 | convolution fusion | flops 1363146240 | bytes 47523840 | tf_op jit(solution)/shard_map/qhd,khd->hqk/dot_general | solution.py:72
  514.1 17.8 %fusion = f32[10,256]{1,0:T(8,128)} fusion(f32[10,256,4096]{2,1,0:T(8,128)} %get-tuple-element.57, f32[10,256]{1,0:T(8,128)S(1)} %get-tuple-element.47), kind=kLoop, calls=%fused_computation.2 | loop fusion | flops 31454720 | bytes 41963520 | tf_op jit(solution)/shard_map/reduce_sum | solution.py:78
  532.0 16.8 %fusion.20 = bf16[256,10,64]{0,2,1:T(8,128)(2,1)} fusion(bf16[4096,10,64]{0,2,1:T(8,128)(2,1)S(1)} %bitcast.113, f32[10,256,4096]{2,1,0:T(8,128)} %get-tuple-element.57, f32[10,256]{1,0:T(8,128)} %copy-done.12, f32[256,10]{0,1:T(8,128)} %bitcast.117, f32[256,10]{0,1:T(8,128)} %get-tuple-element.46), kind=kOutput, calls=%fused_computation.41 | convolution fusion | flops 1374126080 | bytes 47544320 | tf_op jit(solution)/shard_map/hqk,khd->qhd/dot_general | solution.py:79
  548.8 2.3 convolution_add_fusion
  551.3 2.0 fusion.69
  (167 shorter events, 72.4 us)
Async XLA Ops:
  6.5 332.9 %copy-start = (bf16[640,640]{1,0:T(8,128)(2,1)S(1)}, bf16[640,640]{1,0:T(8,128)(2,1)}, u32[]{:S(2)}) copy-start(bf16[640,640]{1,0:T(8,128)(2,1)} %param.35) | copy-start | bytes 2457604
  79.3 8.1 %collective-permute-start.1 = (bf16[8,1,4,640]{3,2,1,0:T(4,128)(2,1)S(1)}, bf16[8,1,4,640]{3,2,1,0:T(4,128)(2,1)S(1)}, u32[]{:S(2)}, u32[]{:S(2)}) collective-permute-start(bf16[8,1,4,640]{3,2,1,0:T(4,128)(2,1)S(1)} %get-tuple-element.45), channel_id=1, source_target_pairs={{16,0},{32,16},{48,32},{64,48},{80,64},{96,80},{112,96},{17,1},{33... | collective-permute-start | bytes 122888 | tf_op jit(solution)/shard_map/ppermute | solution.py:19
  80.6 6.8 %collective-permute-start = (bf16[8,1,4,640]{3,2,1,0:T(4,128)(2,1)S(1)}, bf16[8,1,4,640]{3,2,1,0:T(4,128)(2,1)S(1)}, u32[]{:S(2)}, u32[]{:S(2)}) collective-permute-start(bf16[8,1,4,640]{3,2,1,0:T(4,128)(2,1)S(1)} %get-tuple-element.44), channel_id=1, source_target_pairs={{0,16},{16,32},{32,48},{48,64},{64,80},{80,96},{96,112},{1,17},{17... | collective-permute-start | bytes 122888 | tf_op jit(solution)/shard_map/ppermute | solution.py:16
  88.7 6.8 %collective-permute-start.2 = (bf16[8,10,1,640]{3,2,1,0:T(2,128)(2,1)}, bf16[8,10,1,640]{3,2,1,0:T(2,128)(2,1)S(1)}, u32[]{:S(2)}, u32[]{:S(2)}) collective-permute-start(bf16[8,10,1,640]{3,2,1,0:T(2,128)(2,1)} %get-tuple-element.36), channel_id=1, source_target_pairs={{0,1},{1,2},{2,3},{3,4},{4,5},{5,6},{6,7},{7,8},{8,9},{9,10},{10,1... | collective-permute-start | bytes 307208 | tf_op jit(solution)/shard_map/ppermute | solution.py:16
  91.4 7.4 %collective-permute-start.3 = (bf16[8,10,1,640]{3,2,1,0:T(2,128)(2,1)}, bf16[8,10,1,640]{3,2,1,0:T(2,128)(2,1)}, u32[]{:S(2)}, u32[]{:S(2)}) collective-permute-start(bf16[8,10,1,640]{3,2,1,0:T(2,128)(2,1)} %get-tuple-element.37), channel_id=1, source_target_pairs={{1,0},{2,1},{3,2},{4,3},{5,4},{6,5},{7,6},{8,7},{9,8},{10,9},{11,1... | collective-permute-start | bytes 307208 | tf_op jit(solution)/shard_map/ppermute | solution.py:19
  118.6 91.6 %copy-start.13 = (f32[8,640]{1,0:T(8,128)S(1)}, f32[8,640]{1,0:T(8,128)}, u32[]{:S(2)}) copy-start(f32[8,640]{1,0:T(8,128)} %param.28) | copy-start | bytes 61444
  118.6 91.6 %copy-start.14 = (f32[640]{0:T(1024)S(1)}, f32[640]{0:T(1024)}, u32[]{:S(2)}) copy-start(f32[640]{0:T(1024)} %param.27) | copy-start | bytes 7684
  118.6 91.6 %copy-start.15 = (f32[640]{0:T(1024)S(1)}, f32[640]{0:T(1024)}, u32[]{:S(2)}) copy-start(f32[640]{0:T(1024)} %param.30) | copy-start | bytes 7684
  118.6 91.6 %copy-start.16 = (f32[640]{0:T(1024)S(1)}, f32[640]{0:T(1024)}, u32[]{:S(2)}) copy-start(f32[640]{0:T(1024)} %param.29) | copy-start | bytes 7684
  211.8 8.8 %collective-permute-start.5 = (bf16[8,1,4,640]{3,2,1,0:T(4,128)(2,1)S(1)}, bf16[8,1,4,640]{3,2,1,0:T(4,128)(2,1)S(1)}, u32[]{:S(2)}, u32[]{:S(2)}) collective-permute-start(bf16[8,1,4,640]{3,2,1,0:T(4,128)(2,1)S(1)} %get-tuple-element.41), channel_id=1, source_target_pairs={{16,0},{32,16},{48,32},{64,48},{80,64},{96,80},{112,96},{17,1},{33... | collective-permute-start | bytes 122888 | tf_op jit(solution)/shard_map/ppermute | solution.py:19
  213.1 7.5 %collective-permute-start.4 = (bf16[8,1,4,640]{3,2,1,0:T(4,128)(2,1)S(1)}, bf16[8,1,4,640]{3,2,1,0:T(4,128)(2,1)S(1)}, u32[]{:S(2)}, u32[]{:S(2)}) collective-permute-start(bf16[8,1,4,640]{3,2,1,0:T(4,128)(2,1)S(1)} %get-tuple-element.40), channel_id=1, source_target_pairs={{0,16},{16,32},{32,48},{48,64},{64,80},{80,96},{96,112},{1,17},{17... | collective-permute-start | bytes 122888 | tf_op jit(solution)/shard_map/ppermute | solution.py:16
  222.0 8.5 %collective-permute-start.6 = (bf16[8,10,1,640]{3,2,1,0:T(2,128)(2,1)}, bf16[8,10,1,640]{3,2,1,0:T(2,128)(2,1)}, u32[]{:S(2)}, u32[]{:S(2)}) collective-permute-start(bf16[8,10,1,640]{3,2,1,0:T(2,128)(2,1)} %get-tuple-element.32), channel_id=1, source_target_pairs={{0,1},{1,2},{2,3},{3,4},{4,5},{5,6},{6,7},{7,8},{8,9},{9,10},{10,1... | collective-permute-start | bytes 307208 | tf_op jit(solution)/shard_map/ppermute | solution.py:16
  226.5 7.4 %collective-permute-start.7 = (bf16[8,10,1,640]{3,2,1,0:T(2,128)(2,1)}, bf16[8,10,1,640]{3,2,1,0:T(2,128)(2,1)}, u32[]{:S(2)}, u32[]{:S(2)}) collective-permute-start(bf16[8,10,1,640]{3,2,1,0:T(2,128)(2,1)} %get-tuple-element.33), channel_id=1, source_target_pairs={{1,0},{2,1},{3,2},{4,3},{5,4},{6,5},{7,6},{8,7},{9,8},{10,9},{11,1... | collective-permute-start | bytes 307208 | tf_op jit(solution)/shard_map/ppermute | solution.py:19
  237.6 18.1 %copy-start.3 = (f32[256,640]{1,0:T(8,128)S(1)}, f32[256,640]{1,0:T(8,128)}, u32[]{:S(2)}) copy-start(f32[256,640]{1,0:T(8,128)} %copy-done.2) | copy-start | bytes 1966084
  250.3 7.2 %copy-start.6 = (bf16[256,640]{1,0:T(8,128)(2,1)S(1)}, bf16[256,640]{1,0:T(8,128)(2,1)}, u32[]{:S(2)}) copy-start(bf16[256,640]{1,0:T(8,128)(2,1)} %reshape.203) | copy-start | bytes 983044
  250.3 8.9 %copy-start.7 = (bf16[256,640]{1,0:T(8,128)(2,1)S(1)}, bf16[256,640]{1,0:T(8,128)(2,1)}, u32[]{:S(2)}) copy-start(bf16[256,640]{1,0:T(8,128)(2,1)} %reshape.204) | copy-start | bytes 983044
  252.2 8.6 %copy-start.5 = (f32[256,640]{1,0:T(8,128)S(1)}, f32[256,640]{1,0:T(8,128)}, u32[]{:S(2)}) copy-start(f32[256,640]{1,0:T(8,128)} %fusion.23) | copy-start | bytes 1966084
  257.5 82.0 %copy-start.20 = (f32[640]{0:T(1024)S(1)}, f32[640]{0:T(1024)}, u32[]{:S(2)}) copy-start(f32[640]{0:T(1024)} %param.36) | copy-start | bytes 7684
  257.5 82.0 %copy-start.21 = (f32[640]{0:T(1024)S(1)}, f32[640]{0:T(1024)}, u32[]{:S(2)}) copy-start(f32[640]{0:T(1024)} %param.34) | copy-start | bytes 7684
  257.5 82.0 %copy-start.22 = (f32[640]{0:T(1024)S(1)}, f32[640]{0:T(1024)}, u32[]{:S(2)}) copy-start(f32[640]{0:T(1024)} %param.33) | copy-start | bytes 7684
  257.5 82.8 %copy-start.18 = (f32[640]{0:T(1024)S(1)}, f32[640]{0:T(1024)}, u32[]{:S(2)}) copy-start(f32[640]{0:T(1024)} %param.38) | copy-start | bytes 7684
  257.5 82.8 %copy-start.19 = (f32[640]{0:T(1024)S(1)}, f32[640]{0:T(1024)}, u32[]{:S(2)}) copy-start(f32[640]{0:T(1024)} %param.37) | copy-start | bytes 7684
  262.6 83.1 %copy-start.8 = (bf16[640,640]{1,0:T(8,128)(2,1)S(1)}, bf16[640,640]{1,0:T(8,128)(2,1)}, u32[]{:S(2)}) copy-start(bf16[640,640]{1,0:T(8,128)(2,1)} %param.39) | copy-start | bytes 2457604
  263.8 75.6 %all-to-all-start = ((bf16[8,8,4,640]{3,2,1,0:T(4,128)(2,1)}), bf16[8,8,4,640]{3,2,1,0:T(4,128)(2,1)S(1)}, u32[]{:S(2)}, u32[]{:S(2)}) async-start(bf16[8,8,4,640]{3,2,1,0:T(4,128)(2,1)} %get-tuple-element.17), calls=%async_computation | async-start | bytes 655360 | tf_op jit(solution)/shard_map/all_to_all | solution.py:124
  267.2 133.6 %all-gather.5.cloned.1.call-start = ((), (), s32[]{:S(2)}) async-start(), calls=%async_computation.2 | async-start | bytes 5570560 | tf_op jit(solution)/shard_map/all_gather | solution.py:162
  343.0 118.0 %all-gather.3.cloned.1.call-start = ((), (), s32[]{:S(2)}) async-start(), calls=%async_computation.1 | async-start | bytes 5570560 | tf_op jit(solution)/shard_map/all_gather | solution.py:161
  480.0 52.0 %slice-start = ((s8[5242880]{0:T(1024)(128)(4,1)}), s8[1048576]{0:T(1024)(128)(4,1)S(1)}, s32[]{:S(2)}) async-start(s8[5242880]{0:T(1024)(128)(4,1)} %bitcast.112), calls=%async_computation.3 | async-start | bytes 2097152
  494.6 37.3 %slice-start.1 = ((s8[5242880]{0:T(1024)(128)(4,1)}), s8[4194304]{0:T(1024)(128)(4,1)S(1)}, s32[]{:S(2)}) async-start(s8[5242880]{0:T(1024)(128)(4,1)} %bitcast.112), calls=%async_computation.4 | async-start | bytes 8388608
  514.1 17.8 %copy-start.12 = (f32[10,256]{1,0:T(8,128)}, f32[10,256]{1,0:T(8,128)S(1)}, u32[]{:S(2)}) copy-start(f32[10,256]{1,0:T(8,128)S(1)} %get-tuple-element.47) | copy-start | bytes 30724
  532.0 16.8 %copy-start.23 = (f32[640]{0:T(1024)S(1)}, f32[640]{0:T(1024)}, u32[]{:S(2)}) copy-start(f32[640]{0:T(1024)} %param.45) | copy-start | bytes 7684
  532.0 16.8 %copy-start.24 = (f32[640]{0:T(1024)S(1)}, f32[640]{0:T(1024)}, u32[]{:S(2)}) copy-start(f32[640]{0:T(1024)} %param.43) | copy-start | bytes 7684
  532.0 21.3 %copy-start.1 = (bf16[640,640]{1,0:T(8,128)(2,1)S(1)}, bf16[640,640]{1,0:T(8,128)(2,1)}, u32[]{:S(2)}) copy-start(bf16[640,640]{1,0:T(8,128)(2,1)} %param.35) | copy-start | bytes 2457604
  (6 other events, 31.1 us)
Sparse Core Ops, SparseCore 0:
  343.1 57.6 all-gather.4
  403.3 57.6 all-gather.2
where the time goes:
time: 571 us; the launch traced here: 561 us
  blocking collectives  221 us (39%)
  local copies, waits for them, and re-layouts  104 us (18%)
  waiting for transfers between devices  86.8 us (15%)
  matrix products  73.1 us (13%)
  other arithmetic  35.7 us (6%)
  starting transfers between devices  25.3 us (4%)
  between operations  14.7 us (3%)
    psum x2, blocking collectives, tile_norm(): totals = lax.psum((first_sum, second_sum), ('row', 'col'))  149 us
    psum x1, blocking collectives, shards(): totals = lax.psum((whole_first, whole_second), ('row', 'col'))  71.2 us
    all_gather x1, waiting for transfers between devices, shards(): lax.all_gather(values, 'col', axis=1, tiled=True).reshape(-1, channels)  53.5 us
    dot_general x18, matrix products, convolve(): jnp.dot(window.reshape(-1, channels), weight[shift_row, shift_col], prefe...  30.9 us
    all_gather x1, waiting for transfers between devices, shards(): lax.all_gather(keys, 'col', axis=1, tiled=True).reshape(-1, channels)  26.6 us
    all_gather x1, local copies, waits for them, and re-layouts, shards(): lax.all_gather(values, 'col', axis=1, tiled=True).reshape(-1, channels)  19 us
    all_gather x1, local copies, waits for them, and re-layouts, shards(): lax.all_gather(keys, 'col', axis=1, tiled=True).reshape(-1, channels)  19 us
    dot_general x1, matrix products, absorb(): jnp.einsum('qhd,khd->hqk', query_heads, key_heads, preferred_element_type...  18.9 us
  transfers between devices with their start and end apart: 11, of which 4 were waited for; matrix products, arithmetic and copies ran while one was open for 9% of the time, Pallas kernels for 0%

commit v1 on v0

v1 whole, which is shorter than its diff:
```python
import jax
import jax.numpy as jnp
from jax import lax
from jax.experimental import pallas as pl
from jax.experimental.pallas import tpu as pltpu
from jax.sharding import PartitionSpec as P

MESH = pl.DeviceIdType.MESH
F32 = jnp.float32
BF16 = jnp.bfloat16
C = 640
ROWS = 64
OWN = 4
CELLS = 64 * 64 * 20
LANES = 128
UNITS = 10
ORDER = [(0, 0), (0, 1), (1, 0), (0, 3), (1, 1), (0, 2), (1, 3), (1, 2)]
STAGES = [
    [("own", 0), ("own", 1)],
    [("own", 2), ("own", 3), ("sib", 0), ("sib", 1)],
    [("own", 4), ("own", 5), ("sib", 2), ("sib", 3)],
    [("own", 6), ("own", 7), ("sib", 4), ("sib", 5)],
    [("sib", 6), ("sib", 7)],
]


def dot(a, b):
    return jnp.dot(a, b, preferred_element_type=F32)


def kernel(
    lat, conv1_w, conv2_w, in_w, q_w, k_w, v_w, out_w, proj_w,
    gn1_g, gn1_b, conv1_b, tshift, gn2_g, gn2_b, conv2_b, gn3_g, gn3_b,
    in_b, ln_g, ln_b, out_b, proj_b,
    result,
    w1, w2, wd, group, xin, xcol, stats, parts, taps, conv, resnet, inner,
    qpack, kv, qbuf, queries, kvbuf, vstage, accum, highest, opack, back,
    wsem, a2a_s, a2a_r, halo_s, halo_r, st_s, st_r, q_s, q_r, kv_s, kv_r, fw_s, fw_r, o_s, o_r,
):
    row = lax.axis_index("row")
    col = lax.axis_index("col")
    plane, z, core = lax.div(col, 8), lax.rem(lax.div(col, 2), 4), lax.rem(col, 2)

    def remote(src, dst, send, recv, where):
        return pltpu.make_async_remote_copy(
            src_ref=src, dst_ref=dst, send_sem=send, recv_sem=recv,
            device_id=where, device_id_type=MESH,
        )

    loads = []

    def load(src, dst):
        copy = pltpu.make_async_copy(src, dst, wsem.at[len(loads)])
        copy.start()
        loads.append(copy)

    for source, target in ((conv1_w, w1), (conv2_w, w2)):
        for dx in range(3):
            for dy in range(3):
                load(source.at[dy, dx], target.at[dx, pl.ds(dy * C, C)])
    for i, source in enumerate((in_w, q_w, k_w, v_w, out_w, proj_w)):
        load(source, wd.at[i])

    barrier = pltpu.get_barrier_semaphore()
    for t in range(1, 8):
        pl.semaphore_signal(
            barrier, inc=1, device_id=(lax.rem(row + t, 8), col), device_id_type=MESH
        )
    for t in range(1, 16):
        pl.semaphore_signal(
            barrier, inc=1, device_id=(row, lax.rem(col + t, 16)), device_id_type=MESH
        )
    one = lax.shift_right_logical(lax.broadcasted_iota(jnp.int32, (C, C), 0) * 52429, 20)
    two = lax.shift_right_logical(lax.broadcasted_iota(jnp.int32, (C, C), 1) * 52429, 20)
    group[...] = jnp.where(one == two, 1.0, 0.0).astype(BF16)
    parts[...] = jnp.zeros_like(parts)
    xin[pl.ds(row, 1)] = lat[pl.ds(row, 1)]
    pl.semaphore_wait(barrier, 22)

    swaps = []
    for t in range(1, 8):
        to, frm = lax.rem(row + t, 8), lax.rem(row + 8 - t, 8)
        copy = remote(lat.at[to], xin.at[row], a2a_s.at[t], a2a_r.at[t], (to, col))
        copy.start()
        swaps.append(copy)
    arrived = [
        remote(lat.at[0], xin.at[lax.rem(row + 8 - t, 8)], a2a_s.at[t], a2a_r.at[t], (lax.rem(row + t, 8), col))
        for t in range(1, 8)
    ]
    for copy in arrived:
        copy.wait_recv()
    first = jnp.zeros((8, C), F32)
    second = jnp.zeros((8, C), F32)
    for i in range(4):
        upper = xin[2 * i].astype(F32)
        lower = xin[2 * i + 1].astype(F32)
        for j in range(OWN):
            a, b = upper[8 * j : 8 * j + 8], lower[8 * j : 8 * j + 8]
            first = first + a + b
            second = second + a * a + b * b
            xcol[2 + j, 16 * i : 16 * i + 16, :] = jnp.concatenate([a, b], axis=0).astype(BF16)

    right, left = lax.rem(col + 1, 16), lax.rem(col + 15, 16)
    halos = [
        remote(xcol.at[pl.ds(4, 2)], xcol.at[pl.ds(0, 2)], halo_s.at[0], halo_r.at[0], (row, right)),
        remote(xcol.at[pl.ds(2, 2)], xcol.at[pl.ds(6, 2)], halo_s.at[1], halo_r.at[1], (row, left)),
    ]
    sums = []

    def send_sums(phase, first, second):
        stats[phase, pl.ds(col, 1)] = jnp.concatenate(
            [jnp.sum(first, axis=0, keepdims=True), jnp.sum(second, axis=0, keepdims=True)], axis=0
        )[None]
        for t in range(1, 16):
            copy = remote(
                stats.at[phase, col], stats.at[phase, col], st_s.at[phase, t], st_r.at[phase, t],
                (row, lax.rem(col + t, 16)),
            )
            copy.start()
            sums.append(copy)

    def take_sums(phase, gain, bias, epsilon):
        for t in range(1, 16):
            remote(
                stats.at[phase, col], stats.at[phase, lax.rem(col + 16 - t, 16)],
                st_s.at[phase, t], st_r.at[phase, t], (row, lax.rem(col + t, 16)),
            ).wait_recv()
        total = jnp.sum(stats[phase], axis=0)
        high = total.astype(BF16).astype(F32)
        rest = total - high
        middle = rest.astype(BF16).astype(F32)
        parts[0:2] = high
        parts[2:4] = middle
        parts[4:6] = rest - middle
        spread = dot(parts[...].astype(BF16), group[...])
        mean = (spread[0:1] + spread[2:3] + spread[4:5]) * (1.0 / CELLS)
        square = (spread[1:2] + spread[3:4] + spread[5:6]) * (1.0 / CELLS)
        scale = lax.rsqrt(square - mean * mean + epsilon) * gain[...]
        return scale, bias[...] - mean * scale

    def put_taps(place, values, scale, shift, column):
        v = values * scale + shift
        act = 0.5 * v * (1.0 + jnp.tanh(0.5 * v))
        act = jnp.where((column >= 0) & (column < 64), act, 0.0)
        index = lax.broadcasted_iota(jnp.int32, (ROWS, C), 0)
        above = jnp.where(index == 0, 0.0, pltpu.roll(act, 1, 0))
        below = jnp.where(index == ROWS - 1, 0.0, pltpu.roll(act, ROWS - 1, 0))
        taps[pl.ds(place, 1), :, 0:C] = above.astype(BF16)[None]
        taps[pl.ds(place, 1), :, C : 2 * C] = act.astype(BF16)[None]
        taps[pl.ds(place, 1), :, 2 * C : 3 * C] = below.astype(BF16)[None]

    for copy in halos:
        copy.start()
    send_sums(0, first, second)
    scale1, shift1 = take_sums(0, gn1_g, gn1_b, 1e-5)
    for copy in halos:
        copy.wait_recv()

    @pl.loop(0, 8)
    def _(j):
        values = xcol[pl.ds(j, 1)].reshape(ROWS, C).astype(F32)
        put_taps(j, values, scale1, shift1, 4 * col - 2 + j)

    for copy in loads[:9]:
        copy.wait()
    conv[...] = jnp.broadcast_to(conv1_b[...] + tshift[pl.ds(row, 1), :], conv.shape)

    @pl.loop(0, 3)
    def _(dx):
        lhs = taps[pl.ds(dx, 6)].reshape(6 * ROWS, 3 * C)
        conv[...] += dot(lhs, w1[pl.ds(dx, 1)].reshape(3 * C, C))

    own = conv[ROWS : 5 * ROWS, :].reshape(32, 8, C)
    send_sums(1, jnp.sum(own, axis=0), jnp.sum(own * own, axis=0))
    scale2, shift2 = take_sums(1, gn2_g, gn2_b, 1e-5)

    @pl.loop(0, 6)
    def _(j):
        values = conv[pl.ds(pl.multiple_of(j * ROWS, ROWS), ROWS), :]
        put_taps(j, values, scale2, shift2, 4 * col - 1 + j)

    for copy in loads[9:18]:
        copy.wait()
    conv[0 : 4 * ROWS, :] = xcol[2:6].reshape(4 * ROWS, C).astype(F32) + conv2_b[...]

    @pl.loop(0, 3)
    def _(dx):
        lhs = taps[pl.ds(dx, 4)].reshape(4 * ROWS, 3 * C)
        conv[0 : 4 * ROWS, :] += dot(lhs, w2[pl.ds(dx, 1)].reshape(3 * C, C))

    resnet[...] = conv[0 : 4 * ROWS, :].astype(BF16)
    rounded = resnet[...].astype(F32).reshape(32, 8, C)
    send_sums(2, jnp.sum(rounded, axis=0), jnp.sum(rounded * rounded, axis=0))
    for copy in loads[18:]:
        copy.wait()
    scale3, shift3 = take_sums(2, gn3_g, gn3_b, 1e-6)

    attn_in = (resnet[...].astype(F32) * scale3 + shift3).astype(BF16)
    inner[...] = (dot(attn_in, wd[0]) + in_b[...]).astype(BF16)
    v = inner[...].astype(F32)
    centered = v - jnp.mean(v, axis=-1, keepdims=True)
    variance = jnp.mean(centered * centered, axis=-1, keepdims=True)
    normed = (centered * lax.rsqrt(variance + 1e-5) * ln_g[...] + ln_b[...]).astype(BF16)

    half = lax.broadcasted_iota(jnp.int32, (128, LANES), 1) < 64
    half2 = lax.broadcasted_iota(jnp.int32, (256, LANES), 1) < 64

    def swap(a):
        return pltpu.roll(a, 64, 1)

    q = dot(normed, wd[1]).astype(BF16).astype(F32) * 0.125
    for i in range(5):
        a, b = q[0:128, i * LANES : (i + 1) * LANES], q[128:256, i * LANES : (i + 1) * LANES]
        qpack[2 * i] = jnp.where(half, a, swap(b)).astype(BF16)
        qpack[2 * i + 1] = jnp.where(half, swap(a), b).astype(BF16)

    def place_of(head):
        unit = 16 * (head % 5) + col
        return (head // 5) * 8 + lax.div(unit, 20) * 2 + core, lax.div(lax.rem(unit, 20), 2)

    for head in range(10):
        to, slot = place_of(head)
        copy = remote(qpack.at[head], qbuf.at[slot], q_s.at[head], q_r.at[slot], (row, to))

        @pl.when(to != col)
        def _():
            copy.start()

        @pl.when(to == col)
        def _():
            qbuf[pl.ds(slot, 1)] = qpack[head][None]

    keys = dot(normed, wd[2])
    values = dot(normed, wd[3])
    for i in range(5):
        a, b = keys[:, i * LANES : (i + 1) * LANES], values[:, i * LANES : (i + 1) * LANES]
        kv[2 * i] = jnp.where(half2, a, swap(b)).astype(BF16)
        kv[2 * i + 1] = jnp.where(half2, swap(a), b).astype(BF16)

    def chip(dx, dz):
        return lax.rem(plane + dx, 2), lax.rem(z + dz, 4)

    here = plane * 4 + z
    kvbuf[pl.ds(core, 1), pl.ds(here, 1)] = kv[pl.ds(5 * plane + z, 2)][None, None]
    spreads = []
    for t, (dx, dz) in enumerate(ORDER):
        if t == 0:
            continue
        p2, z2 = chip(dx, dz)
        copy = remote(
            kv.at[pl.ds(5 * p2 + z2, 2)], kvbuf.at[core, here], kv_s.at[t], kv_r.at[t],
            (row, p2 * 8 + z2 * 2 + core),
        )
        copy.start()
        spreads.append(copy)

    sibling = (row, plane * 8 + z * 2 + 1 - core)

    def source(t):
        dx, dz = ORDER[t]
        p2, z2 = chip(dx, 4 - dz)
        return p2 * 4 + z2

    def unit_of(j):
        unit = 20 * z + 2 * j + core
        head, block = lax.div(unit, 16), lax.rem(unit, 16)
        return head, block

    for j in range(UNITS):
        head, block = unit_of(j)

        @pl.when(block != col)
        def _():
            remote(qpack.at[0], qbuf.at[j], q_s.at[0], q_r.at[j], (row, block)).wait_recv()

    @pl.loop(0, UNITS)
    def _(j):
        packed = qbuf[pl.ds(j, 1)].reshape(128, LANES).astype(F32)
        low = jnp.where(half, packed, 0.0).astype(BF16)
        high = jnp.where(half, swap(packed), 0.0).astype(BF16)
        queries[pl.ds(j, 1)] = jnp.concatenate([low, high], axis=0)[None]

    lane = lax.broadcasted_iota(jnp.int32, (1, LANES), 1)
    keep = jnp.where(lane < 64, 0.0, 1.0).astype(BF16)
    ones = jnp.where(lane < 64, 1.0, 0.0).astype(BF16)
    forwards, returns = [], []
    for number, blocks in enumerate(STAGES):
        start, end = number == 0, number == len(STAGES) - 1
        width = 256 * len(blocks)
        slots = []
        for kind, t in blocks:
            g = source(t)
            if kind == "own":
                if t:
                    remote(
                        kv.at[pl.ds(0, 2)], kvbuf.at[core, g], kv_s.at[t], kv_r.at[t], sibling
                    ).wait_recv()
                copy = remote(kvbuf.at[core, g], kvbuf.at[core, g], fw_s.at[t], fw_r.at[t], sibling)
                copy.start()
                forwards.append(copy)
                slots.append((core, g))
        for kind, t in blocks:
            g = source(t)
            if kind == "sib":
                remote(
                    kvbuf.at[core, g], kvbuf.at[1 - core, g], fw_s.at[t], fw_r.at[t], sibling
                ).wait_recv()
                slots.append((1 - core, g))
        for head in range(2):
            for i, (parity, g) in enumerate(slots):
                block = kvbuf[pl.ds(parity, 1), pl.ds(g, 1), head].reshape(256, LANES)
                vstage[0, head, 256 * i : 256 * i + 256, :] = block
                vstage[1, head, 256 * i : 256 * i + 256, :] = block * keep + ones

        @pl.loop(0, UNITS)
        def _(j):
            head, block = unit_of(j)
            slot = head - z
            packed = []
            for part in range(2):
                rows = pl.ds(128 * part, 128)
                q = queries[pl.ds(j, 1), rows].reshape(128, LANES)
                k = vstage[0, pl.ds(slot, 1), 0:width].reshape(width, LANES)
                v = vstage[1, pl.ds(slot, 1), 0:width].reshape(width, LANES)
                scores = lax.dot_general(
                    q, k, (((1,), (1,)), ((), ())), preferred_element_type=F32
                )
                most = jnp.broadcast_to(jnp.max(scores, axis=1, keepdims=True), (128, LANES))
                if not start:
                    before = highest[pl.ds(j, 1), rows].reshape(128, LANES)
                    most = jnp.maximum(most, before)
                expo = jnp.exp(scores - jnp.concatenate([most] * (width // LANES), axis=1))
                total = dot(expo.astype(BF16), v)
                if not start:
                    total += accum[pl.ds(j, 1), rows].reshape(128, LANES) * jnp.exp(before - most)
                if end:
                    packed.append(total / swap(total))
                else:
                    highest[pl.ds(j, 1), rows] = most[None]
                    accum[pl.ds(j, 1), rows] = total[None]
            if end:
                opack[pl.ds(j, 1)] = jnp.where(half, swap(packed[0]), packed[1]).astype(BF16)[None]
                whole = 5 * plane + head

                @pl.when(block != col)
                def _():
                    remote(
                        opack.at[j], back.at[whole], o_s.at[j], o_r.at[whole], (row, block)
                    ).start()

                @pl.when(block == col)
                def _():
                    back[pl.ds(whole, 1)] = opack[pl.ds(j, 1)]

    for head in range(10):
        frm, slot = place_of(head)

        @pl.when(frm != col)
        def _():
            remote(opack.at[0], back.at[head], o_s.at[0], o_r.at[head], (row, frm)).wait_recv()

    tiles = []
    for i in range(5):
        a, b = back[2 * i].astype(F32), back[2 * i + 1].astype(F32)
        tiles.append(
            jnp.concatenate([jnp.where(half, a, swap(b)), jnp.where(half, swap(a), b)], axis=0)
        )
    attended = jnp.concatenate(tiles, axis=1).astype(BF16)
    mixed = (inner[...].astype(F32) + dot(attended, wd[4]) + out_b[...]).astype(BF16)
    result[...] = (resnet[...].astype(F32) + dot(mixed, wd[5]) + proj_b[...]).astype(BF16)

    for copy in swaps + halos + sums + spreads + forwards:
        copy.wait_send()
    for head in range(10):
        to, slot = place_of(head)

        @pl.when(to != col)
        def _():
            remote(qpack.at[head], qbuf.at[slot], q_s.at[head], q_r.at[slot], (row, to)).wait_send()

    for j in range(UNITS):
        head, block = unit_of(j)

        @pl.when(block != col)
        def _():
            remote(opack.at[j], back.at[0], o_s.at[j], o_r.at[0], (row, block)).wait_send()


def shards(
    latent, gn1_gain, gn1_bias, conv1_weight, conv1_bias, time_shift, gn2_gain, gn2_bias,
    conv2_weight, conv2_bias, gn3_gain, gn3_bias, in_weight, in_bias, ln_gain, ln_bias,
    query_weight, key_weight, value_weight, out_weight, out_bias, proj_weight, proj_bias,
):
    lat = latent.transpose(0, 2, 1, 3).reshape(8, 32, C)
    vec = lambda a: a.reshape(1, C)
    hbm = pl.BlockSpec(memory_space=pl.ANY)
    vmem = pl.BlockSpec(memory_space=pltpu.VMEM)
    dma = pltpu.SemaphoreType.DMA
    result = pl.pallas_call(
        kernel,
        out_shape=jax.ShapeDtypeStruct((OWN * ROWS, C), BF16),
        in_specs=[vmem] + [hbm] * 8 + [vmem] * 14,
        out_specs=vmem,
        scratch_shapes=[
            pltpu.VMEM((3, 3 * C, C), BF16),
            pltpu.VMEM((3, 3 * C, C), BF16),
            pltpu.VMEM((6, C, C), BF16),
            pltpu.VMEM((C, C), BF16),
            pltpu.VMEM((8, 32, C), BF16),
            pltpu.VMEM((8, ROWS, C), BF16),
            pltpu.VMEM((3, 16, 2, C), F32),
            pltpu.VMEM((8, C), F32),
            pltpu.VMEM((8, ROWS, 3 * C), BF16),
            pltpu.VMEM((6 * ROWS, C), F32),
            pltpu.VMEM((256, C), BF16),
            pltpu.VMEM((256, C), BF16),
            pltpu.VMEM((10, 128, LANES), BF16),
            pltpu.VMEM((10, 256, LANES), BF16),
            pltpu.VMEM((UNITS, 128, LANES), BF16),
            pltpu.VMEM((UNITS, 256, LANES), BF16),
            pltpu.VMEM((2, 8, 2, 256, LANES), BF16),
            pltpu.VMEM((2, 2, 1024, LANES), BF16),
            pltpu.VMEM((UNITS, 256, LANES), F32),
            pltpu.VMEM((UNITS, 256, LANES), F32),
            pltpu.VMEM((UNITS, 128, LANES), BF16),
            pltpu.VMEM((10, 128, LANES), BF16),
            dma((24,)), dma((8,)), dma((8,)), dma((2,)), dma((2,)), dma((3, 16)), dma((3, 16)),
            dma((10,)), dma((10,)), dma((8,)), dma((8,)), dma((8,)), dma((8,)),
            dma((10,)), dma((10,)),
        ],
        compiler_params=pltpu.CompilerParams(
            collective_id=0, has_side_effects=True, vmem_limit_bytes=56 * 2**20
        ),
        cost_estimate=pl.CostEstimate(
            flops=8 * 10**9, bytes_accessed=21 * 10**6, transcendentals=11 * 10**6
        ),
    )(
        lat, conv1_weight, conv2_weight, in_weight, query_weight, key_weight, value_weight,
        out_weight, proj_weight, vec(gn1_gain), vec(gn1_bias), vec(conv1_bias), time_shift,
        vec(gn2_gain), vec(gn2_bias), vec(conv2_bias), vec(gn3_gain), vec(gn3_bias),
        vec(in_bias), vec(ln_gain), vec(ln_bias), vec(out_bias), vec(proj_bias),
    )
    return result.reshape(OWN, ROWS, C).transpose(1, 0, 2)[None]


def solution(mesh):
    placed = (P(None, "row", "col", None),) + (P(),) * 22
    return jax.shard_map(
        shards, mesh=mesh, in_specs=placed, out_specs=P("row", None, "col", None), check_vma=False
    )
```

time: 571 us -> 124 us (0.22)
  the two profiles are of different devices: /device:TPU:1 before, /device:TPU:6 now
where the time goes in v1:
time: 124 us; the launch traced here: 123 us
  Pallas kernels  103 us (83%)
  local copies, waits for them, and re-layouts  20.3 us (16%)
    pallas_call x1, Pallas kernels, shards(): pl.pallas_call(kernel, out_shape=jax.ShapeDtypeStruct((OWN * ROWS, C), BF...  103 us
    reshape x13, local copies, waits for them, and re-layouts, shards(): vec = lambda a: a.reshape(1, C)  16.6 us

profile of v1, /device:TPU:6, one launch (start us, length us, event | category | flops | bytes accessed | tf_op | source)
XLA Modules:
  0.0 123.2 jit_solution(648596256970152026)
XLA Ops:
  0.0 1.3 %reshape.46.gn1_g = f32[1,640]{1,0:T(1,128)} reshape(f32[640]{0:T(1024)} %param.24) | data formatting | bytes 5120 | tf_op jit(solution)/shard_map/reshape | solution.py:395
  1.3 1.3 %reshape.47.gn1_b = f32[1,640]{1,0:T(1,128)} reshape(f32[640]{0:T(1024)} %param.25) | data formatting | bytes 5120 | tf_op jit(solution)/shard_map/reshape | solution.py:395
  2.6 1.3 %reshape.48.conv1_b = f32[1,640]{1,0:T(1,128)} reshape(f32[640]{0:T(1024)} %param.27) | data formatting | bytes 5120 | tf_op jit(solution)/shard_map/reshape | solution.py:395
  3.8 1.3 %reshape.49.gn2_g = f32[1,640]{1,0:T(1,128)} reshape(f32[640]{0:T(1024)} %param.29) | data formatting | bytes 5120 | tf_op jit(solution)/shard_map/reshape | solution.py:395
  5.1 1.3 %reshape.50.gn2_b = f32[1,640]{1,0:T(1,128)} reshape(f32[640]{0:T(1024)} %param.30) | data formatting | bytes 5120 | tf_op jit(solution)/shard_map/reshape | solution.py:395
  6.4 1.3 %reshape.51.conv2_b = f32[1,640]{1,0:T(1,128)} reshape(f32[640]{0:T(1024)} %param.32) | data formatting | bytes 5120 | tf_op jit(solution)/shard_map/reshape | solution.py:395
  7.6 1.3 %reshape.52.gn3_g = f32[1,640]{1,0:T(1,128)} reshape(f32[640]{0:T(1024)} %param.33) | data formatting | bytes 5120 | tf_op jit(solution)/shard_map/reshape | solution.py:395
  8.9 1.3 %reshape.53.gn3_b = f32[1,640]{1,0:T(1,128)} reshape(f32[640]{0:T(1024)} %param.34) | data formatting | bytes 5120 | tf_op jit(solution)/shard_map/reshape | solution.py:395
  10.2 1.3 %reshape.54.in_b = f32[1,640]{1,0:T(1,128)} reshape(f32[640]{0:T(1024)} %param.36) | data formatting | bytes 5120 | tf_op jit(solution)/shard_map/reshape | solution.py:395
  11.5 1.3 %reshape.55.ln_g = f32[1,640]{1,0:T(1,128)} reshape(f32[640]{0:T(1024)} %param.37) | data formatting | bytes 5120 | tf_op jit(solution)/shard_map/reshape | solution.py:395
  12.7 1.3 %reshape.56.ln_b = f32[1,640]{1,0:T(1,128)} reshape(f32[640]{0:T(1024)} %param.38) | data formatting | bytes 5120 | tf_op jit(solution)/shard_map/reshape | solution.py:395
  14.0 1.3 %reshape.57.out_b = f32[1,640]{1,0:T(1,128)} reshape(f32[640]{0:T(1024)} %param.43) | data formatting | bytes 5120 | tf_op jit(solution)/shard_map/reshape | solution.py:395
  15.3 1.3 %reshape.58.proj_b = f32[1,640]{1,0:T(1,128)} reshape(f32[640]{0:T(1024)} %param.45) | data formatting | bytes 5120 | tf_op jit(solution)/shard_map/reshape | solution.py:395
  16.6 1.7 %copy.29 = bf16[8,4,8,640]{3,2,1,0:T(8,128)(2,1)} copy(bf16[8,4,8,640]{3,1,2,0:T(4,128)(2,1)} %bitcast.10) | data formatting | bytes 655360 | tf_op jit(solution)/shard_map/transpose | solution.py:394
  18.3 102.9 %shard_map.217 = bf16[256,640]{1,0:T(8,128)(2,1)} custom-call(bf16[8,32,640]{2,1,0:T(8,128)(2,1)} %bitcast.12, bf16[3,3,640,640]{3,2,1,0:T(8,128)(2,1)} %conv1_w.1, bf16[3,3,640,640]{3,2,1,0:T(8,128)(2,1)} %conv2_w.1, bf16[640,640]{1,0:T(8,128)(2,1)} %in_w.1, bf16[640,640]{1,0:T(8,128)(2,1)} %q_w.1, bf16[640,640]{1,0:T(8,128)(2,1)} %k_w.1, ...), custom_call_target="tpu_custom_call" | custom-call | flops 8000000000 | bytes 21000000 | tf_op jit(solution)/shard_map/pallas_call | solution.py:399
  121.2 2.0 %copy.28 = bf16[4,64,640]{2,0,1:T(4,128)(2,1)} copy(bf16[4,64,640]{2,1,0:T(8,128)(2,1)} %bitcast.11) | data formatting | bytes 655360 | tf_op jit(solution)/shard_map/reshape | solution.py:443

commit v2 on v1

--- a/solution.py
+++ b/solution.py
@@ -16,11 +16,8 @@
 UNITS = 10
 ORDER = [(0, 0), (0, 1), (1, 0), (0, 3), (1, 1), (0, 2), (1, 3), (1, 2)]
 STAGES = [
-    [("own", 0), ("own", 1)],
-    [("own", 2), ("own", 3), ("sib", 0), ("sib", 1)],
-    [("own", 4), ("own", 5), ("sib", 2), ("sib", 3)],
-    [("own", 6), ("own", 7), ("sib", 4), ("sib", 5)],
-    [("sib", 6), ("sib", 7)],
+    [(kind, t) for kind in ("own", "sib") for t in range(2 * number, 2 * number + 2)]
+    for number in range(4)
 ]
 
 
@@ -47,12 +44,35 @@
             device_id=where, device_id_type=MESH,
         )
 
+    leaving = []
+
+    def send(copy, when=None):
+        def start():
+            copy.start()
+
+        def leave():
+            copy.wait_send()
+
+        if when is None:
+            start()
+            leaving.append(leave)
+        else:
+            pl.when(when)(start)
+            leaving.append(lambda: pl.when(when)(leave))
+
     loads = []
 
     def load(src, dst):
-        copy = pltpu.make_async_copy(src, dst, wsem.at[len(loads)])
+        copy = pltpu.make_async_copy(src, dst, wsem.at[next(used)])
         copy.start()
         loads.append(copy)
+
+    def loaded(count):
+        for copy in loads[:count]:
+            copy.wait()
+        del loads[:count]
+
+    used = iter(range(24))
 
     for source, target in ((conv1_w, w1), (conv2_w, w2)):
         for dx in range(3):
@@ -77,12 +97,9 @@
     xin[pl.ds(row, 1)] = lat[pl.ds(row, 1)]
     pl.semaphore_wait(barrier, 22)
 
-    swaps = []
     for t in range(1, 8):
-        to, frm = lax.rem(row + t, 8), lax.rem(row + 8 - t, 8)
-        copy = remote(lat.at[to], xin.at[row], a2a_s.at[t], a2a_r.at[t], (to, col))
-        copy.start()
-        swaps.append(copy)
+        to = lax.rem(row + t, 8)
+        send(remote(lat.at[to], xin.at[row], a2a_s.at[t], a2a_r.at[t], (to, col)))
     arrived = [
         remote(lat.at[0], xin.at[lax.rem(row + 8 - t, 8)], a2a_s.at[t], a2a_r.at[t], (lax.rem(row + t, 8), col))
         for t in range(1, 8)
@@ -105,19 +122,15 @@
         remote(xcol.at[pl.ds(4, 2)], xcol.at[pl.ds(0, 2)], halo_s.at[0], halo_r.at[0], (row, right)),
         remote(xcol.at[pl.ds(2, 2)], xcol.at[pl.ds(6, 2)], halo_s.at[1], halo_r.at[1], (row, left)),
     ]
-    sums = []
-
     def send_sums(phase, first, second):
         stats[phase, pl.ds(col, 1)] = jnp.concatenate(
             [jnp.sum(first, axis=0, keepdims=True), jnp.sum(second, axis=0, keepdims=True)], axis=0
         )[None]
         for t in range(1, 16):
-            copy = remote(
+            send(remote(
                 stats.at[phase, col], stats.at[phase, col], st_s.at[phase, t], st_r.at[phase, t],
                 (row, lax.rem(col + t, 16)),
-            )
-            copy.start()
-            sums.append(copy)
+            ))
 
     def take_sums(phase, gain, bias, epsilon):
         for t in range(1, 16):
@@ -135,8 +148,8 @@
         spread = dot(parts[...].astype(BF16), group[...])
         mean = (spread[0:1] + spread[2:3] + spread[4:5]) * (1.0 / CELLS)
         square = (spread[1:2] + spread[3:4] + spread[5:6]) * (1.0 / CELLS)
-        scale = lax.rsqrt(square - mean * mean + epsilon) * gain[...]
-        return scale, bias[...] - mean * scale
+        scale = lax.rsqrt(square - mean * mean + epsilon) * gain[...].reshape(1, C)
+        return scale, bias[...].reshape(1, C) - mean * scale
 
     def put_taps(place, values, scale, shift, column):
         v = values * scale + shift
@@ -150,7 +163,7 @@
         taps[pl.ds(place, 1), :, 2 * C : 3 * C] = below.astype(BF16)[None]
 
     for copy in halos:
-        copy.start()
+        send(copy)
     send_sums(0, first, second)
     scale1, shift1 = take_sums(0, gn1_g, gn1_b, 1e-5)
     for copy in halos:
@@ -161,9 +174,8 @@
         values = xcol[pl.ds(j, 1)].reshape(ROWS, C).astype(F32)
         put_taps(j, values, scale1, shift1, 4 * col - 2 + j)
 
-    for copy in loads[:9]:
-        copy.wait()
-    conv[...] = jnp.broadcast_to(conv1_b[...] + tshift[pl.ds(row, 1), :], conv.shape)
+    loaded(9)
+    conv[...] = jnp.broadcast_to(conv1_b[...].reshape(1, C) + tshift[pl.ds(row, 1), :], conv.shape)
 
     @pl.loop(0, 3)
     def _(dx):
@@ -179,9 +191,8 @@
         values = conv[pl.ds(pl.multiple_of(j * ROWS, ROWS), ROWS), :]
         put_taps(j, values, scale2, shift2, 4 * col - 1 + j)
 
-    for copy in loads[9:18]:
-        copy.wait()
-    conv[0 : 4 * ROWS, :] = xcol[2:6].reshape(4 * ROWS, C).astype(F32) + conv2_b[...]
+    loaded(9)
+    conv[0 : 4 * ROWS, :] = xcol[2:6].reshape(4 * ROWS, C).astype(F32) + conv2_b[...].reshape(1, C)
 
     @pl.loop(0, 3)
     def _(dx):
@@ -191,16 +202,15 @@
     resnet[...] = conv[0 : 4 * ROWS, :].astype(BF16)
     rounded = resnet[...].astype(F32).reshape(32, 8, C)
     send_sums(2, jnp.sum(rounded, axis=0), jnp.sum(rounded * rounded, axis=0))
-    for copy in loads[18:]:
-        copy.wait()
+    loaded(6)
     scale3, shift3 = take_sums(2, gn3_g, gn3_b, 1e-6)
 
     attn_in = (resnet[...].astype(F32) * scale3 + shift3).astype(BF16)
-    inner[...] = (dot(attn_in, wd[0]) + in_b[...]).astype(BF16)
+    inner[...] = (dot(attn_in, wd[0]) + in_b[...].reshape(1, C)).astype(BF16)
     v = inner[...].astype(F32)
     centered = v - jnp.mean(v, axis=-1, keepdims=True)
     variance = jnp.mean(centered * centered, axis=-1, keepdims=True)
-    normed = (centered * lax.rsqrt(variance + 1e-5) * ln_g[...] + ln_b[...]).astype(BF16)
+    normed = (centered * lax.rsqrt(variance + 1e-5) * ln_g[...].reshape(1, C) + ln_b[...].reshape(1, C)).astype(BF16)
 
     half = lax.broadcasted_iota(jnp.int32, (128, LANES), 1) < 64
     half2 = lax.broadcasted_iota(jnp.int32, (256, LANES), 1) < 64
@@ -220,11 +230,7 @@
 
     for head in range(10):
         to, slot = place_of(head)
-        copy = remote(qpack.at[head], qbuf.at[slot], q_s.at[head], q_r.at[slot], (row, to))
-
-        @pl.when(to != col)
-        def _():
-            copy.start()
+        send(remote(qpack.at[head], qbuf.at[slot], q_s.at[head], q_r.at[slot], (row, to)), to != col)
 
         @pl.when(to == col)
         def _():
@@ -242,17 +248,14 @@
 
     here = plane * 4 + z
     kvbuf[pl.ds(core, 1), pl.ds(here, 1)] = kv[pl.ds(5 * plane + z, 2)][None, None]
-    spreads = []
     for t, (dx, dz) in enumerate(ORDER):
         if t == 0:
             continue
         p2, z2 = chip(dx, dz)
-        copy = remote(
+        send(remote(
             kv.at[pl.ds(5 * p2 + z2, 2)], kvbuf.at[core, here], kv_s.at[t], kv_r.at[t],
             (row, p2 * 8 + z2 * 2 + core),
-        )
-        copy.start()
-        spreads.append(copy)
+        ))
 
     sibling = (row, plane * 8 + z * 2 + 1 - core)
 
@@ -278,12 +281,11 @@
         packed = qbuf[pl.ds(j, 1)].reshape(128, LANES).astype(F32)
         low = jnp.where(half, packed, 0.0).astype(BF16)
         high = jnp.where(half, swap(packed), 0.0).astype(BF16)
-        queries[pl.ds(j, 1)] = jnp.concatenate([low, high], axis=0)[None]
+        queries[pl.ds(pl.multiple_of(256 * j, 256), 256)] = jnp.concatenate([low, high], axis=0)
 
     lane = lax.broadcasted_iota(jnp.int32, (1, LANES), 1)
     keep = jnp.where(lane < 64, 0.0, 1.0).astype(BF16)
     ones = jnp.where(lane < 64, 1.0, 0.0).astype(BF16)
-    forwards, returns = [], []
     for number, blocks in enumerate(STAGES):
         start, end = number == 0, number == len(STAGES) - 1
         width = 256 * len(blocks)
@@ -295,9 +297,7 @@
                     remote(
                         kv.at[pl.ds(0, 2)], kvbuf.at[core, g], kv_s.at[t], kv_r.at[t], sibling
                     ).wait_recv()
-                copy = remote(kvbuf.at[core, g], kvbuf.at[core, g], fw_s.at[t], fw_r.at[t], sibling)
-                copy.start()
-                forwards.append(copy)
+                send(remote(kvbuf.at[core, g], kvbuf.at[core, g], fw_s.at[t], fw_r.at[t], sibling))
                 slots.append((core, g))
         for kind, t in blocks:
             g = source(t)
@@ -312,45 +312,38 @@
                 vstage[0, head, 256 * i : 256 * i + 256, :] = block
                 vstage[1, head, 256 * i : 256 * i + 256, :] = block * keep + ones
 
-        @pl.loop(0, UNITS)
-        def _(j):
-            head, block = unit_of(j)
-            slot = head - z
-            packed = []
-            for part in range(2):
-                rows = pl.ds(128 * part, 128)
-                q = queries[pl.ds(j, 1), rows].reshape(128, LANES)
-                k = vstage[0, pl.ds(slot, 1), 0:width].reshape(width, LANES)
-                v = vstage[1, pl.ds(slot, 1), 0:width].reshape(width, LANES)
-                scores = lax.dot_general(
-                    q, k, (((1,), (1,)), ((), ())), preferred_element_type=F32
-                )
-                most = jnp.broadcast_to(jnp.max(scores, axis=1, keepdims=True), (128, LANES))
-                if not start:
-                    before = highest[pl.ds(j, 1), rows].reshape(128, LANES)
-                    most = jnp.maximum(most, before)
-                expo = jnp.exp(scores - jnp.concatenate([most] * (width // LANES), axis=1))
-                total = dot(expo.astype(BF16), v)
-                if not start:
-                    total += accum[pl.ds(j, 1), rows].reshape(128, LANES) * jnp.exp(before - most)
-                if end:
-                    packed.append(total / swap(total))
-                else:
-                    highest[pl.ds(j, 1), rows] = most[None]
-                    accum[pl.ds(j, 1), rows] = total[None]
-            if end:
-                opack[pl.ds(j, 1)] = jnp.where(half, swap(packed[0]), packed[1]).astype(BF16)[None]
+        for pair in range(UNITS // 2):
+            rows = slice(512 * pair, 512 * pair + 512)
+            slot = unit_of(2 * pair)[0] - z
+            k = vstage[0, pl.ds(slot, 1), 0:width].reshape(width, LANES)
+            v = vstage[1, pl.ds(slot, 1), 0:width].reshape(width, LANES)
+            scores = lax.dot_general(
+                queries[rows], k, (((1,), (1,)), ((), ())), preferred_element_type=F32
+            )
+            most = jnp.broadcast_to(jnp.max(scores, axis=1, keepdims=True), (512, LANES))
+            if not start:
+                before = highest[rows]
+                most = jnp.maximum(most, before)
+            expo = jnp.exp(scores - jnp.concatenate([most] * (width // LANES), axis=1))
+            total = dot(expo.astype(BF16), v)
+            if not start:
+                total += accum[rows] * jnp.exp(before - most)
+            if not end:
+                highest[rows] = most
+                accum[rows] = total
+                continue
+            total = total / swap(total)
+            for i in range(2):
+                j = 2 * pair + i
+                a, b = total[256 * i : 256 * i + 128], total[256 * i + 128 : 256 * i + 256]
+                opack[j] = jnp.where(half, swap(a), b).astype(BF16)
+                head, block = unit_of(j)
                 whole = 5 * plane + head
-
-                @pl.when(block != col)
-                def _():
-                    remote(
-                        opack.at[j], back.at[whole], o_s.at[j], o_r.at[whole], (row, block)
-                    ).start()
+                send(remote(opack.at[j], back.at[whole], o_s.at[j], o_r.at[whole], (row, block)), block != col)
 
                 @pl.when(block == col)
                 def _():
-                    back[pl.ds(whole, 1)] = opack[pl.ds(j, 1)]
+                    back[pl.ds(whole, 1)] = opack[j][None]
 
     for head in range(10):
         frm, slot = place_of(head)
@@ -366,25 +359,11 @@
             jnp.concatenate([jnp.where(half, a, swap(b)), jnp.where(half, swap(a), b)], axis=0)
         )
     attended = jnp.concatenate(tiles, axis=1).astype(BF16)
-    mixed = (inner[...].astype(F32) + dot(attended, wd[4]) + out_b[...]).astype(BF16)
-    result[...] = (resnet[...].astype(F32) + dot(mixed, wd[5]) + proj_b[...]).astype(BF16)
-
-    for copy in swaps + halos + sums + spreads + forwards:
-        copy.wait_send()
-    for head in range(10):
-        to, slot = place_of(head)
-
-        @pl.when(to != col)
-        def _():
-            remote(qpack.at[head], qbuf.at[slot], q_s.at[head], q_r.at[slot], (row, to)).wait_send()
-
-    for j in range(UNITS):
-        head, block = unit_of(j)
-
-        @pl.when(block != col)
-        def _():
-            remote(opack.at[j], back.at[0], o_s.at[j], o_r.at[0], (row, block)).wait_send()
-
+    mixed = (inner[...].astype(F32) + dot(attended, wd[4]) + out_b[...].reshape(1, C)).astype(BF16)
+    result[...] = (resnet[...].astype(F32) + dot(mixed, wd[5]) + proj_b[...].reshape(1, C)).astype(BF16)
+
+    for leave in leaving:
+        leave()
 
 def shards(
     latent, gn1_gain, gn1_bias, conv1_weight, conv1_bias, time_shift, gn2_gain, gn2_bias,
@@ -392,7 +371,6 @@
     query_weight, key_weight, value_weight, out_weight, out_bias, proj_weight, proj_bias,
 ):
     lat = latent.transpose(0, 2, 1, 3).reshape(8, 32, C)
-    vec = lambda a: a.reshape(1, C)
     hbm = pl.BlockSpec(memory_space=pl.ANY)
     vmem = pl.BlockSpec(memory_space=pltpu.VMEM)
     dma = pltpu.SemaphoreType.DMA
@@ -417,11 +395,11 @@
             pltpu.VMEM((10, 128, LANES), BF16),
             pltpu.VMEM((10, 256, LANES), BF16),
             pltpu.VMEM((UNITS, 128, LANES), BF16),
-            pltpu.VMEM((UNITS, 256, LANES), BF16),
+            pltpu.VMEM((UNITS * 256, LANES), BF16),
             pltpu.VMEM((2, 8, 2, 256, LANES), BF16),
             pltpu.VMEM((2, 2, 1024, LANES), BF16),
-            pltpu.VMEM((UNITS, 256, LANES), F32),
-            pltpu.VMEM((UNITS, 256, LANES), F32),
+            pltpu.VMEM((UNITS * 256, LANES), F32),
+            pltpu.VMEM((UNITS * 256, LANES), F32),
             pltpu.VMEM((UNITS, 128, LANES), BF16),
             pltpu.VMEM((10, 128, LANES), BF16),
             dma((24,)), dma((8,)), dma((8,)), dma((2,)), dma((2,)), dma((3, 16)), dma((3, 16)),
@@ -436,9 +414,9 @@
         ),
     )(
         lat, conv1_weight, conv2_weight, in_weight, query_weight, key_weight, value_weight,
-        out_weight, proj_weight, vec(gn1_gain), vec(gn1_bias), vec(conv1_bias), time_shift,
-        vec(gn2_gain), vec(gn2_bias), vec(conv2_bias), vec(gn3_gain), vec(gn3_bias),
-        vec(in_bias), vec(ln_gain), vec(ln_bias), vec(out_bias), vec(proj_bias),
+        out_weight, proj_weight, gn1_gain, gn1_bias, conv1_bias, time_shift,
+        gn2_gain, gn2_bias, conv2_bias, gn3_gain, gn3_bias,
+        in_bias, ln_gain, ln_bias, out_bias, proj_bias,
     )
     return result.reshape(OWN, ROWS, C).transpose(1, 0, 2)[None]
 

time: 124 us -> 91.1 us (0.73)
  the two profiles are of different devices: /device:TPU:6 before, /device:TPU:1 now
where the time goes in v2:
time: 91.1 us; the launch traced here: 89.5 us
  Pallas kernels  85.8 us (94%)
  local copies, waits for them, and re-layouts  3.68 us (4%)
    pallas_call x1, Pallas kernels, shards(): pl.pallas_call(kernel, out_shape=jax.ShapeDtypeStruct((OWN * ROWS, C), BF...  85.8 us
    reshape x1, local copies, waits for them, and re-layouts, shards(): return result.reshape(OWN, ROWS, C).transpose(1, 0, 2)[None]  1.95 us

profile of v2, /device:TPU:1, one launch (start us, length us, event | category | flops | bytes accessed | tf_op | source)
XLA Modules:
  0.0 89.5 jit_solution(14413567313460288822)
XLA Ops:
  0.0 1.7 %copy.29 = bf16[8,4,8,640]{3,2,1,0:T(8,128)(2,1)} copy(bf16[8,4,8,640]{3,1,2,0:T(4,128)(2,1)} %bitcast.10) | data formatting | bytes 655360 | tf_op jit(solution)/shard_map/transpose | solution.py:373
  1.7 85.8 %shard_map.217 = bf16[256,640]{1,0:T(8,128)(2,1)} custom-call(bf16[8,32,640]{2,1,0:T(8,128)(2,1)} %bitcast.12, bf16[3,3,640,640]{3,2,1,0:T(8,128)(2,1)} %conv1_w.1, bf16[3,3,640,640]{3,2,1,0:T(8,128)(2,1)} %conv2_w.1, bf16[640,640]{1,0:T(8,128)(2,1)} %in_w.1, bf16[640,640]{1,0:T(8,128)(2,1)} %q_w.1, bf16[640,640]{1,0:T(8,128)(2,1)} %k_w.1, ...), custom_call_target="tpu_custom_call" | custom-call | flops 8000000000 | bytes 21000000 | tf_op jit(solution)/shard_map/pallas_call | solution.py:377
  87.6 2.0 %copy.28 = bf16[4,64,640]{2,0,1:T(4,128)(2,1)} copy(bf16[4,64,640]{2,1,0:T(8,128)(2,1)} %bitcast.11) | data formatting | bytes 655360 | tf_op jit(solution)/shard_map/reshape | solution.py:421

commit v3 on v2

--- a/solution.py
+++ b/solution.py
@@ -14,10 +14,10 @@
 CELLS = 64 * 64 * 20
 LANES = 128
 UNITS = 10
-ORDER = [(0, 0), (0, 1), (1, 0), (0, 3), (1, 1), (0, 2), (1, 3), (1, 2)]
+ORDER = [(0, 0), (1, 0), (0, 1), (0, 3), (1, 1), (1, 3), (0, 2), (1, 2)]
 STAGES = [
-    [(kind, t) for kind in ("own", "sib") for t in range(2 * number, 2 * number + 2)]
-    for number in range(4)
+    [(kind, t) for kind in ("own", "sib") for t in chunks]
+    for chunks in ((0,), (1, 2, 3), (4, 5), (6, 7))
 ]
 
 
@@ -30,7 +30,7 @@
     gn1_g, gn1_b, conv1_b, tshift, gn2_g, gn2_b, conv2_b, gn3_g, gn3_b,
     in_b, ln_g, ln_b, out_b, proj_b,
     result,
-    w1, w2, wd, group, xin, xcol, stats, parts, taps, conv, resnet, inner,
+    w1, w2, wd, group, xin, cells, xcol, edge, stats, parts, taps, conv, resnet, inner,
     qpack, kv, qbuf, queries, kvbuf, vstage, accum, highest, opack, back,
     wsem, a2a_s, a2a_r, halo_s, halo_r, st_s, st_r, q_s, q_r, kv_s, kv_r, fw_s, fw_r, o_s, o_r,
 ):
@@ -74,12 +74,12 @@
 
     used = iter(range(24))
 
-    for source, target in ((conv1_w, w1), (conv2_w, w2)):
+    def load_conv(source, target):
         for dx in range(3):
             for dy in range(3):
                 load(source.at[dy, dx], target.at[dx, pl.ds(dy * C, C)])
-    for i, source in enumerate((in_w, q_w, k_w, v_w, out_w, proj_w)):
-        load(source, wd.at[i])
+
+    load_conv(conv1_w, w1)
 
     barrier = pltpu.get_barrier_semaphore()
     for t in range(1, 8):
@@ -106,21 +106,33 @@
     ]
     for copy in arrived:
         copy.wait_recv()
+    load_conv(conv2_w, w2)
+    for i, source in enumerate((in_w, q_w, k_w, v_w, out_w, proj_w)):
+        load(source, wd.at[i])
     first = jnp.zeros((8, C), F32)
     second = jnp.zeros((8, C), F32)
-    for i in range(4):
-        upper = xin[2 * i].astype(F32)
-        lower = xin[2 * i + 1].astype(F32)
-        for j in range(OWN):
-            a, b = upper[8 * j : 8 * j + 8], lower[8 * j : 8 * j + 8]
-            first = first + a + b
-            second = second + a * a + b * b
-            xcol[2 + j, 16 * i : 16 * i + 16, :] = jnp.concatenate([a, b], axis=0).astype(BF16)
+    for i in range(8):
+        for j in range(8):
+            cell = xin[i, j].astype(F32)
+            for k in range(5):
+                cells[k, 32 * i + 4 * j : 32 * i + 4 * j + 4, :] = cell[:, k * LANES : (k + 1) * LANES]
+    for j in range(OWN):
+        column = jnp.concatenate(
+            [cells[k, pl.ds(j, ROWS, stride=OWN), :] for k in range(5)], axis=1
+        )
+        xcol[1 + j] = column.astype(BF16)
+        column = column.reshape(8, 8, C)
+        first = first + jnp.sum(column, axis=0)
+        second = second + jnp.sum(column * column, axis=0)
 
     right, left = lax.rem(col + 1, 16), lax.rem(col + 15, 16)
     halos = [
-        remote(xcol.at[pl.ds(4, 2)], xcol.at[pl.ds(0, 2)], halo_s.at[0], halo_r.at[0], (row, right)),
-        remote(xcol.at[pl.ds(2, 2)], xcol.at[pl.ds(6, 2)], halo_s.at[1], halo_r.at[1], (row, left)),
+        remote(xcol.at[4], xcol.at[0], halo_s.at[0], halo_r.at[0], (row, right)),
+        remote(xcol.at[1], xcol.at[5], halo_s.at[1], halo_r.at[1], (row, left)),
+    ]
+    borders = [
+        remote(edge.at[1], edge.at[2], halo_s.at[2], halo_r.at[2], (row, right)),
+        remote(edge.at[0], edge.at[3], halo_s.at[3], halo_r.at[3], (row, left)),
     ]
     def send_sums(phase, first, second):
         stats[phase, pl.ds(col, 1)] = jnp.concatenate(
@@ -169,37 +181,49 @@
     for copy in halos:
         copy.wait_recv()
 
-    @pl.loop(0, 8)
+    @pl.loop(0, 6)
     def _(j):
         values = xcol[pl.ds(j, 1)].reshape(ROWS, C).astype(F32)
-        put_taps(j, values, scale1, shift1, 4 * col - 2 + j)
+        put_taps(j, values, scale1, shift1, 4 * col - 1 + j)
 
     loaded(9)
     conv[...] = jnp.broadcast_to(conv1_b[...].reshape(1, C) + tshift[pl.ds(row, 1), :], conv.shape)
-
-    @pl.loop(0, 3)
-    def _(dx):
-        lhs = taps[pl.ds(dx, 6)].reshape(6 * ROWS, 3 * C)
-        conv[...] += dot(lhs, w1[pl.ds(dx, 1)].reshape(3 * C, C))
-
-    own = conv[ROWS : 5 * ROWS, :].reshape(32, 8, C)
-    send_sums(1, jnp.sum(own, axis=0), jnp.sum(own * own, axis=0))
-    scale2, shift2 = take_sums(1, gn2_g, gn2_b, 1e-5)
-
-    @pl.loop(0, 6)
-    def _(j):
-        values = conv[pl.ds(pl.multiple_of(j * ROWS, ROWS), ROWS), :]
-        put_taps(j, values, scale2, shift2, 4 * col - 1 + j)
-
-    loaded(9)
-    conv[0 : 4 * ROWS, :] = xcol[2:6].reshape(4 * ROWS, C).astype(F32) + conv2_b[...].reshape(1, C)
 
     @pl.loop(0, 3)
     def _(dx):
         lhs = taps[pl.ds(dx, 4)].reshape(4 * ROWS, 3 * C)
-        conv[0 : 4 * ROWS, :] += dot(lhs, w2[pl.ds(dx, 1)].reshape(3 * C, C))
-
-    resnet[...] = conv[0 : 4 * ROWS, :].astype(BF16)
+        conv[...] += dot(lhs, w1[pl.ds(dx, 1)].reshape(3 * C, C))
+
+    edge[0] = conv[0:ROWS, :].astype(BF16)
+    edge[1] = conv[3 * ROWS : 4 * ROWS, :].astype(BF16)
+    for copy in borders:
+        send(copy)
+    own = conv[...].reshape(32, 8, C)
+    send_sums(1, jnp.sum(own, axis=0), jnp.sum(own * own, axis=0))
+    scale2, shift2 = take_sums(1, gn2_g, gn2_b, 1e-5)
+
+    @pl.loop(0, 4)
+    def _(j):
+        values = conv[pl.ds(pl.multiple_of(j * ROWS, ROWS), ROWS), :]
+        put_taps(j + 1, values, scale2, shift2, 4 * col + j)
+
+    for copy in borders:
+        copy.wait_recv()
+
+    @pl.loop(0, 2)
+    def _(j):
+        values = edge[pl.ds(2 + j, 1)].reshape(ROWS, C).astype(F32)
+        put_taps(5 * j, values, scale2, shift2, 4 * col - 1 + 5 * j)
+
+    loaded(9)
+    conv[...] = xcol[1:5].reshape(4 * ROWS, C).astype(F32) + conv2_b[...].reshape(1, C)
+
+    @pl.loop(0, 3)
+    def _(dx):
+        lhs = taps[pl.ds(dx, 4)].reshape(4 * ROWS, 3 * C)
+        conv[...] += dot(lhs, w2[pl.ds(dx, 1)].reshape(3 * C, C))
+
+    resnet[...] = conv[...].astype(BF16)
     rounded = resnet[...].astype(F32).reshape(32, 8, C)
     send_sums(2, jnp.sum(rounded, axis=0), jnp.sum(rounded * rounded, axis=0))
     loaded(6)
@@ -218,24 +242,6 @@
     def swap(a):
         return pltpu.roll(a, 64, 1)
 
-    q = dot(normed, wd[1]).astype(BF16).astype(F32) * 0.125
-    for i in range(5):
-        a, b = q[0:128, i * LANES : (i + 1) * LANES], q[128:256, i * LANES : (i + 1) * LANES]
-        qpack[2 * i] = jnp.where(half, a, swap(b)).astype(BF16)
-        qpack[2 * i + 1] = jnp.where(half, swap(a), b).astype(BF16)
-
-    def place_of(head):
-        unit = 16 * (head % 5) + col
-        return (head // 5) * 8 + lax.div(unit, 20) * 2 + core, lax.div(lax.rem(unit, 20), 2)
-
-    for head in range(10):
-        to, slot = place_of(head)
-        send(remote(qpack.at[head], qbuf.at[slot], q_s.at[head], q_r.at[slot], (row, to)), to != col)
-
-        @pl.when(to == col)
-        def _():
-            qbuf[pl.ds(slot, 1)] = qpack[head][None]
-
     keys = dot(normed, wd[2])
     values = dot(normed, wd[3])
     for i in range(5):
@@ -248,14 +254,36 @@
 
     here = plane * 4 + z
     kvbuf[pl.ds(core, 1), pl.ds(here, 1)] = kv[pl.ds(5 * plane + z, 2)][None, None]
-    for t, (dx, dz) in enumerate(ORDER):
-        if t == 0:
-            continue
-        p2, z2 = chip(dx, dz)
-        send(remote(
-            kv.at[pl.ds(5 * p2 + z2, 2)], kvbuf.at[core, here], kv_s.at[t], kv_r.at[t],
-            (row, p2 * 8 + z2 * 2 + core),
-        ))
+
+    def send_keys(number):
+        for kind, t in STAGES[number]:
+            if kind == "sib" or t == 0:
+                continue
+            p2, z2 = chip(*ORDER[t])
+            send(remote(
+                kv.at[pl.ds(5 * p2 + z2, 2)], kvbuf.at[core, here], kv_s.at[t], kv_r.at[t],
+                (row, p2 * 8 + z2 * 2 + core),
+            ))
+
+    send_keys(1)
+
+    q = dot(normed, wd[1]).astype(BF16).astype(F32) * 0.125
+    for i in range(5):
+        a, b = q[0:128, i * LANES : (i + 1) * LANES], q[128:256, i * LANES : (i + 1) * LANES]
+        qpack[2 * i] = jnp.where(half, a, swap(b)).astype(BF16)
+        qpack[2 * i + 1] = jnp.where(half, swap(a), b).astype(BF16)
+
+    def place_of(head):
+        unit = 16 * (head % 5) + col
+        return (head // 5) * 8 + lax.div(unit, 20) * 2 + core, lax.div(lax.rem(unit, 20), 2)
+
+    for head in range(10):
+        to, slot = place_of(head)
+        send(remote(qpack.at[head], qbuf.at[slot], q_s.at[head], q_r.at[slot], (row, to)), to != col)
+
+        @pl.when(to == col)
+        def _():
+            qbuf[pl.ds(slot, 1)] = qpack[head][None]
 
     sibling = (row, plane * 8 + z * 2 + 1 - core)
 
@@ -269,19 +297,21 @@
         head, block = lax.div(unit, 16), lax.rem(unit, 16)
         return head, block
 
-    for j in range(UNITS):
-        head, block = unit_of(j)
-
-        @pl.when(block != col)
-        def _():
-            remote(qpack.at[0], qbuf.at[j], q_s.at[0], q_r.at[j], (row, block)).wait_recv()
-
-    @pl.loop(0, UNITS)
-    def _(j):
-        packed = qbuf[pl.ds(j, 1)].reshape(128, LANES).astype(F32)
-        low = jnp.where(half, packed, 0.0).astype(BF16)
-        high = jnp.where(half, swap(packed), 0.0).astype(BF16)
-        queries[pl.ds(pl.multiple_of(256 * j, 256), 256)] = jnp.concatenate([low, high], axis=0)
+    def take_queries():
+        for j in range(UNITS):
+            head, block = unit_of(j)
+
+            @pl.when(block != col)
+            def _():
+                remote(qpack.at[0], qbuf.at[j], q_s.at[0], q_r.at[j], (row, block)).wait_recv()
+
+        send_keys(2)
+        @pl.loop(0, UNITS)
+        def _(j):
+            packed = qbuf[pl.ds(j, 1)].reshape(128, LANES).astype(F32)
+            low = jnp.where(half, packed, 0.0).astype(BF16)
+            high = jnp.where(half, swap(packed), 0.0).astype(BF16)
+            queries[pl.ds(pl.multiple_of(256 * j, 256), 256)] = jnp.concatenate([low, high], axis=0)
 
     lane = lax.broadcasted_iota(jnp.int32, (1, LANES), 1)
     keep = jnp.where(lane < 64, 0.0, 1.0).astype(BF16)
@@ -299,6 +329,8 @@
                     ).wait_recv()
                 send(remote(kvbuf.at[core, g], kvbuf.at[core, g], fw_s.at[t], fw_r.at[t], sibling))
                 slots.append((core, g))
+        if number == 1:
+            send_keys(3)
         for kind, t in blocks:
             g = source(t)
             if kind == "sib":
@@ -312,6 +344,8 @@
                 vstage[0, head, 256 * i : 256 * i + 256, :] = block
                 vstage[1, head, 256 * i : 256 * i + 256, :] = block * keep + ones
 
+        if start:
+            take_queries()
         for pair in range(UNITS // 2):
             rows = slice(512 * pair, 512 * pair + 512)
             slot = unit_of(2 * pair)[0] - z
@@ -370,7 +404,6 @@
     conv2_weight, conv2_bias, gn3_gain, gn3_bias, in_weight, in_bias, ln_gain, ln_bias,
     query_weight, key_weight, value_weight, out_weight, out_bias, proj_weight, proj_bias,
 ):
-    lat = latent.transpose(0, 2, 1, 3).reshape(8, 32, C)
     hbm = pl.BlockSpec(memory_space=pl.ANY)
     vmem = pl.BlockSpec(memory_space=pltpu.VMEM)
     dma = pltpu.SemaphoreType.DMA
@@ -384,12 +417,14 @@
             pltpu.VMEM((3, 3 * C, C), BF16),
             pltpu.VMEM((6, C, C), BF16),
             pltpu.VMEM((C, C), BF16),
-            pltpu.VMEM((8, 32, C), BF16),
-            pltpu.VMEM((8, ROWS, C), BF16),
+            pltpu.VMEM((8, 8, OWN, C), BF16),
+            pltpu.VMEM((5, OWN * ROWS, LANES), F32),
+            pltpu.VMEM((6, ROWS, C), BF16),
+            pltpu.VMEM((4, ROWS, C), BF16),
             pltpu.VMEM((3, 16, 2, C), F32),
             pltpu.VMEM((8, C), F32),
-            pltpu.VMEM((8, ROWS, 3 * C), BF16),
-            pltpu.VMEM((6 * ROWS, C), F32),
+            pltpu.VMEM((6, ROWS, 3 * C), BF16),
+            pltpu.VMEM((OWN * ROWS, C), F32),
             pltpu.VMEM((256, C), BF16),
             pltpu.VMEM((256, C), BF16),
             pltpu.VMEM((10, 128, LANES), BF16),
@@ -397,12 +432,12 @@
             pltpu.VMEM((UNITS, 128, LANES), BF16),
             pltpu.VMEM((UNITS * 256, LANES), BF16),
             pltpu.VMEM((2, 8, 2, 256, LANES), BF16),
-            pltpu.VMEM((2, 2, 1024, LANES), BF16),
+            pltpu.VMEM((2, 2, 1536, LANES), BF16),
             pltpu.VMEM((UNITS * 256, LANES), F32),
             pltpu.VMEM((UNITS * 256, LANES), F32),
             pltpu.VMEM((UNITS, 128, LANES), BF16),
             pltpu.VMEM((10, 128, LANES), BF16),
-            dma((24,)), dma((8,)), dma((8,)), dma((2,)), dma((2,)), dma((3, 16)), dma((3, 16)),
+            dma((24,)), dma((8,)), dma((8,)), dma((4,)), dma((4,)), dma((3, 16)), dma((3, 16)),
             dma((10,)), dma((10,)), dma((8,)), dma((8,)), dma((8,)), dma((8,)),
             dma((10,)), dma((10,)),
         ],
@@ -413,7 +448,7 @@
             flops=8 * 10**9, bytes_accessed=21 * 10**6, transcendentals=11 * 10**6
         ),
     )(
-        lat, conv1_weight, conv2_weight, in_weight, query_weight, key_weight, value_weight,
+        latent, conv1_weight, conv2_weight, in_weight, query_weight, key_weight, value_weight,
         out_weight, proj_weight, gn1_gain, gn1_bias, conv1_bias, time_shift,
         gn2_gain, gn2_bias, conv2_bias, gn3_gain, gn3_bias,
         in_bias, ln_gain, ln_bias, out_bias, proj_bias,

time: 91.1 us -> 83.6 us (0.918); the launches traced: 89.5 us -> 83.2 us
  Pallas kernels: 85.8 us -> 81.3 us
  local copies, waits for them, and re-layouts: 3.68 us -> 1.95 us
    pallas_call x1, Pallas kernels: 85.8 us -> 81.3 us  [shards(): pl.pallas_call(kernel, out_shape=jax.ShapeDtypeStruct((OWN * ROWS, C), BF...]
    transpose x1 -> x0, local copies, waits for them, and re-layouts: 1.73 us -> none  [shards(): lat = latent.transpose(0, 2, 1, 3).reshape(8, 32, C)]
where the time goes in v3:
time: 83.6 us; the launch traced here: 83.2 us
  Pallas kernels  81.3 us (97%)
  local copies, waits for them, and re-layouts  1.95 us (2%)
    pallas_call x1, Pallas kernels, shards(): pl.pallas_call(kernel, out_shape=jax.ShapeDtypeStruct((OWN * ROWS, C), BF...  81.3 us
    reshape x1, local copies, waits for them, and re-layouts, shards(): return result.reshape(OWN, ROWS, C).transpose(1, 0, 2)[None]  1.95 us

profile of v3, /device:TPU:1, one launch (start us, length us, event | category | flops | bytes accessed | tf_op | source)
XLA Modules:
  0.0 83.2 jit_solution(2514690349503970823)
XLA Ops:
  0.0 81.3 %shard_map.217 = bf16[256,640]{1,0:T(8,128)(2,1)} custom-call(bf16[8,8,4,640]{3,2,1,0:T(4,128)(2,1)} %lat.1, bf16[3,3,640,640]{3,2,1,0:T(8,128)(2,1)} %conv1_w.1, bf16[3,3,640,640]{3,2,1,0:T(8,128)(2,1)} %conv2_w.1, bf16[640,640]{1,0:T(8,128)(2,1)} %in_w.1, bf16[640,640]{1,0:T(8,128)(2,1)} %q_w.1, bf16[640,640]{1,0:T(8,128)(2,1)} %k_w.1, ...), custom_call_target="tpu_custom_call" | custom-call | flops 8000000000 | bytes 21000000 | tf_op jit(solution)/shard_map/pallas_call | solution.py:410
  81.3 2.0 %copy.26 = bf16[4,64,640]{2,0,1:T(4,128)(2,1)} copy(bf16[4,64,640]{2,1,0:T(8,128)(2,1)} %bitcast.6) | data formatting | bytes 655360 | tf_op jit(solution)/shard_map/reshape | solution.py:456

commit v4 on v3

--- a/solution.py
+++ b/solution.py
@@ -17,7 +17,7 @@
 ORDER = [(0, 0), (1, 0), (0, 1), (0, 3), (1, 1), (1, 3), (0, 2), (1, 2)]
 STAGES = [
     [(kind, t) for kind in ("own", "sib") for t in chunks]
-    for chunks in ((0,), (1, 2, 3), (4, 5), (6, 7))
+    for chunks in ((0,), (1, 2, 3), (4, 5, 6), (7,))
 ]
 
 
@@ -79,8 +79,6 @@
             for dy in range(3):
                 load(source.at[dy, dx], target.at[dx, pl.ds(dy * C, C)])
 
-    load_conv(conv1_w, w1)
-
     barrier = pltpu.get_barrier_semaphore()
     for t in range(1, 8):
         pl.semaphore_signal(
@@ -90,16 +88,17 @@
         pl.semaphore_signal(
             barrier, inc=1, device_id=(row, lax.rem(col + t, 16)), device_id_type=MESH
         )
+    pl.semaphore_wait(barrier, 22)
+
+    for t in range(1, 8):
+        to = lax.rem(row + t, 8)
+        send(remote(lat.at[to], xin.at[row], a2a_s.at[t], a2a_r.at[t], (to, col)))
+    load_conv(conv1_w, w1)
     one = lax.shift_right_logical(lax.broadcasted_iota(jnp.int32, (C, C), 0) * 52429, 20)
     two = lax.shift_right_logical(lax.broadcasted_iota(jnp.int32, (C, C), 1) * 52429, 20)
     group[...] = jnp.where(one == two, 1.0, 0.0).astype(BF16)
     parts[...] = jnp.zeros_like(parts)
     xin[pl.ds(row, 1)] = lat[pl.ds(row, 1)]
-    pl.semaphore_wait(barrier, 22)
-
-    for t in range(1, 8):
-        to = lax.rem(row + t, 8)
-        send(remote(lat.at[to], xin.at[row], a2a_s.at[t], a2a_r.at[t], (to, col)))
     arrived = [
         remote(lat.at[0], xin.at[lax.rem(row + 8 - t, 8)], a2a_s.at[t], a2a_r.at[t], (lax.rem(row + t, 8), col))
         for t in range(1, 8)
@@ -242,6 +241,24 @@
     def swap(a):
         return pltpu.roll(a, 64, 1)
 
+    q = dot(normed, wd[1]).astype(BF16).astype(F32) * 0.125
+    for i in range(5):
+        a, b = q[0:128, i * LANES : (i + 1) * LANES], q[128:256, i * LANES : (i + 1) * LANES]
+        qpack[2 * i] = jnp.where(half, a, swap(b)).astype(BF16)
+        qpack[2 * i + 1] = jnp.where(half, swap(a), b).astype(BF16)
+
+    def place_of(head):
+        unit = 16 * (head % 5) + col
+        return (head // 5) * 8 + lax.div(unit, 20) * 2 + core, lax.div(lax.rem(unit, 20), 2)
+
+    for head in range(10):
+        to, slot = place_of(head)
+        send(remote(qpack.at[head], qbuf.at[slot], q_s.at[head], q_r.at[slot], (row, to)), to != col)
+
+        @pl.when(to == col)
+        def _():
+            qbuf[pl.ds(slot, 1)] = qpack[head][None]
+
     keys = dot(normed, wd[2])
     values = dot(normed, wd[3])
     for i in range(5):
@@ -266,24 +283,6 @@
             ))
 
     send_keys(1)
-
-    q = dot(normed, wd[1]).astype(BF16).astype(F32) * 0.125
-    for i in range(5):
-        a, b = q[0:128, i * LANES : (i + 1) * LANES], q[128:256, i * LANES : (i + 1) * LANES]
-        qpack[2 * i] = jnp.where(half, a, swap(b)).astype(BF16)
-        qpack[2 * i + 1] = jnp.where(half, swap(a), b).astype(BF16)
-
-    def place_of(head):
-        unit = 16 * (head % 5) + col
-        return (head // 5) * 8 + lax.div(unit, 20) * 2 + core, lax.div(lax.rem(unit, 20), 2)
-
-    for head in range(10):
-        to, slot = place_of(head)
-        send(remote(qpack.at[head], qbuf.at[slot], q_s.at[head], q_r.at[slot], (row, to)), to != col)
-
-        @pl.when(to == col)
-        def _():
-            qbuf[pl.ds(slot, 1)] = qpack[head][None]
 
     sibling = (row, plane * 8 + z * 2 + 1 - core)
 
@@ -341,16 +340,21 @@
         for head in range(2):
             for i, (parity, g) in enumerate(slots):
                 block = kvbuf[pl.ds(parity, 1), pl.ds(g, 1), head].reshape(256, LANES)
-                vstage[0, head, 256 * i : 256 * i + 256, :] = block
-                vstage[1, head, 256 * i : 256 * i + 256, :] = block * keep + ones
+                vstage[head, 256 * i : 256 * i + 256, :] = block * keep + ones
 
         if start:
             take_queries()
         for pair in range(UNITS // 2):
             rows = slice(512 * pair, 512 * pair + 512)
             slot = unit_of(2 * pair)[0] - z
-            k = vstage[0, pl.ds(slot, 1), 0:width].reshape(width, LANES)
-            v = vstage[1, pl.ds(slot, 1), 0:width].reshape(width, LANES)
+            k = jnp.concatenate(
+                [
+                    kvbuf[pl.ds(parity, 1), pl.ds(g, 1), pl.ds(slot, 1)].reshape(256, LANES)
+                    for parity, g in slots
+                ],
+                axis=0,
+            )
+            v = vstage[pl.ds(slot, 1), 0:width].reshape(width, LANES)
             scores = lax.dot_general(
                 queries[rows], k, (((1,), (1,)), ((), ())), preferred_element_type=F32
             )
@@ -432,7 +436,7 @@
             pltpu.VMEM((UNITS, 128, LANES), BF16),
             pltpu.VMEM((UNITS * 256, LANES), BF16),
             pltpu.VMEM((2, 8, 2, 256, LANES), BF16),
-            pltpu.VMEM((2, 2, 1536, LANES), BF16),
+            pltpu.VMEM((2, 1536, LANES), BF16),
             pltpu.VMEM((UNITS * 256, LANES), F32),
             pltpu.VMEM((UNITS * 256, LANES), F32),
             pltpu.VMEM((UNITS, 128, LANES), BF16),

time: 83.6 us -> 81.7 us (0.977)
  the two profiles are of different devices: /device:TPU:1 before, /device:TPU:13 now
where the time goes in v4:
time: 81.7 us; the launch traced here: 81.5 us
  Pallas kernels  79.5 us (97%)
  local copies, waits for them, and re-layouts  1.95 us (2%)
    pallas_call x1, Pallas kernels, shards(): pl.pallas_call(kernel, out_shape=jax.ShapeDtypeStruct((OWN * ROWS, C), BF...  79.5 us
    reshape x1, local copies, waits for them, and re-layouts, shards(): return result.reshape(OWN, ROWS, C).transpose(1, 0, 2)[None]  1.95 us

profile of v4, /device:TPU:13, one launch (start us, length us, event | category | flops | bytes accessed | tf_op | source)
XLA Modules:
  0.0 81.5 jit_solution(4811032419037096164)
XLA Ops:
  0.0 79.5 %shard_map.217 = bf16[256,640]{1,0:T(8,128)(2,1)} custom-call(bf16[8,8,4,640]{3,2,1,0:T(4,128)(2,1)} %lat.1, bf16[3,3,640,640]{3,2,1,0:T(8,128)(2,1)} %conv1_w.1, bf16[3,3,640,640]{3,2,1,0:T(8,128)(2,1)} %conv2_w.1, bf16[640,640]{1,0:T(8,128)(2,1)} %in_w.1, bf16[640,640]{1,0:T(8,128)(2,1)} %q_w.1, bf16[640,640]{1,0:T(8,128)(2,1)} %k_w.1, ...), custom_call_target="tpu_custom_call" | custom-call | flops 8000000000 | bytes 21000000 | tf_op jit(solution)/shard_map/pallas_call | solution.py:414
  79.6 2.0 %copy.26 = bf16[4,64,640]{2,0,1:T(4,128)(2,1)} copy(bf16[4,64,640]{2,1,0:T(8,128)(2,1)} %bitcast.6) | data formatting | bytes 655360 | tf_op jit(solution)/shard_map/reshape | solution.py:460
